TPU v7x, 256 devices: a whole 4x4x8 slice. The times are simulated.
256 devices in a mesh: pair: 16 (over y_hi, z), row: 4 (over x), col: 4 (over y_lo, core).
Axes of the slice: x: 4, y: 4 (y_hi: 2, y_lo: 2; y = y_hi * 2 + y_lo), z: 8, core: 2. Of those that a mesh axis runs over, the one named last changes fastest.
Arguments:
- psi_val: bfloat16 [32, 786432], P(None, ('row', 'col')), may hold values from -6 to 6
- psi_con: bfloat16 [64, 786432], P(None, ('row', 'col')), may hold values from -6 to 6
- e_val: float32 [32], replicated, may hold values from -12 to -2
- e_con: float32 [64], replicated, may hold values from 1 to 10
- val_idx: int32 [512], P('pair'), may hold values from 0 to 31
- con_idx: int32 [512], P('pair'), may hold values from 0 to 63
- gmap: int32 [4096], replicated, may hold values from 0 to 786431, as said below
Outputs:
- chi: float32 [4096, 4096], P(('pair', 'row'), 'col')
Inputs may be any that keep to these rules, and one draw needn't show every extreme that they name: `gmap`: distinct grid indices; both 0 and 786431 occur.
All inputs are finite; a program needn't handle non-finite values.
Results may differ from a plain program's by a relative error of at most 0.0059.
Values may be sent and summed in bfloat16 or wider, within the bound.
No kernel may reach another device: no remote copies, remote signals or barrier semaphores. Data moves between devices by JAX's collectives and lax.ppermute only.
A program may use at most 192 MiB of HBM per device.

v0:
```python
import math

import jax
import jax.numpy as jnp
from jax import lax
from jax.sharding import PartitionSpec as P

NG = 4096
GX = 64
GY = 64
GZ = 192


def angle_table(length):
    indices = jnp.arange(length, dtype=jnp.int32)
    product = indices[:, None] * indices[None, :] % length
    angles = 2.0 * math.pi / length * product.astype(jnp.float32)
    return (jnp.cos(angles), jnp.sin(angles))


def yz_spectrum(grid):
    items, planes, side_y, side_z = grid.shape
    high = lax.Precision.HIGHEST
    cos_z, sin_z = angle_table(side_z)
    table_z = jnp.stack((cos_z, -sin_z), axis=1)
    after_z = jnp.einsum("mayz,zsk->maysk", grid, table_z, precision=high)
    cos_y, sin_y = angle_table(side_y)
    first_row = jnp.stack((cos_y, -sin_y), axis=1)
    second_row = jnp.stack((sin_y, cos_y), axis=1)
    table_y = jnp.stack((first_row, second_row), axis=1)
    after_y = jnp.einsum("maysk,ystj->matjk", after_z, table_y, precision=high)
    return after_y.reshape(items, planes, 2, side_y * side_z)


def x_finish(picked, plane_ids, outer_ids, side_x):
    items = picked.shape[0]
    angles = (
        2.0
        * math.pi
        / side_x
        * (plane_ids[:, None] * outer_ids[None, :] % side_x).astype(jnp.float32)
    )
    cosine_table = jnp.cos(angles)[None, :, :]
    sine_table = jnp.sin(angles)[None, :, :]
    real_part = picked[:, :, 0, :]
    imag_part = picked[:, :, 1, :]
    out_real = jnp.sum(cosine_table * real_part + sine_table * imag_part, axis=1)
    out_imag = jnp.sum(cosine_table * imag_part - sine_table * real_part, axis=1)
    return jnp.stack((out_real, out_imag), axis=2).reshape(items, 2 * outer_ids.shape[0])


def contract_last(left, right):
    return lax.dot_general(
        left, right, (((1,), (1,)), ((), ())), preferred_element_type=jnp.float32
    )


def body(psi_val, psi_con, e_val, e_con, val_idx, con_idx, gmap):
    pair_rows = val_idx.shape[0]
    local_points = psi_val.shape[1]
    pair_count = lax.axis_size("pair")
    row_count = lax.axis_size("row")
    col_count = lax.axis_size("col")
    grid_devices = row_count * col_count
    row_here = lax.axis_index("row")
    col_here = lax.axis_index("col")
    densities = (
        jnp.take(psi_val, val_idx, axis=0).astype(jnp.float32)
        * jnp.take(psi_con, con_idx, axis=0).astype(jnp.float32)
    ).astype(jnp.bfloat16)
    weights = -2.0 / (
        math.sqrt(pair_rows * pair_count) * (jnp.take(e_con, con_idx) - jnp.take(e_val, val_idx))
    )
    factor = 1.0 / math.sqrt(GX * GY * GZ)
    plane_size = GY * GZ
    inner_ids = gmap % plane_size
    outer_ids = gmap // plane_size
    sub_rows = NG // (pair_count * row_count)
    col_width = NG // col_count
    per_device = pair_rows // grid_devices
    grouped_rows = densities.reshape(grid_devices, per_device, local_points)
    all_planes = jnp.arange(GX, dtype=jnp.int32)

    def one_grid(single):
        spectrum = yz_spectrum(single.reshape(1, GX, GY, GZ).astype(jnp.float32))
        picked = jnp.take(spectrum, inner_ids, axis=3)
        return x_finish(picked, all_planes, outer_ids, GX)[0]

    received = lax.all_to_all(grouped_rows, ("row", "col"), split_axis=0, concat_axis=2, tiled=True)
    items = received.shape[1]
    grids = received.reshape(items, GX * GY * GZ)
    stacked = lax.map(one_grid, grids) * factor
    own_columns = stacked.T.astype(jnp.bfloat16)
    coefficients = lax.all_gather(own_columns, ("row", "col"), axis=1, tiled=True)
    grouped = coefficients.reshape(pair_count, row_count, 2 * sub_rows, pair_rows)
    row_part = lax.dynamic_index_in_dim(grouped, row_here, 1, keepdims=False).reshape(
        2 * pair_count * sub_rows, pair_rows
    )
    col_part = lax.dynamic_slice_in_dim(coefficients, col_here * 2 * col_width, 2 * col_width, 0)
    weighted = (
        row_part.astype(jnp.float32).reshape(pair_count * sub_rows, 2, pair_rows)
        * weights[None, None, :]
    ).astype(jnp.bfloat16)
    weighted = weighted.reshape(pair_count * sub_rows, 2 * pair_rows)
    column_side = col_part.reshape(col_width, 2 * pair_rows)
    return lax.psum_scatter(
        contract_last(weighted, column_side), "pair", scatter_dimension=0, tiled=True
    )


def solution(mesh):
    return jax.shard_map(
        body,
        mesh=mesh,
        in_specs=(
            P(None, ("row", "col")),
            P(None, ("row", "col")),
            P(),
            P(),
            P("pair"),
            P("pair"),
            P(),
        ),
        out_specs=P(("pair", "row"), "col"),
        check_vma=False,
    )
```

profile of v0, /device:TPU:2, one launch (start us, length us, event | category | flops | bytes accessed | tf_op | source)
XLA Modules:
  0.0 599.0 jit_solution(7704283321971426901)
XLA Ops:
  6.5 0.0 copy-start
  6.5 0.8 compare_select_fusion.2
  7.4 0.8 compare_and_fusion.1
  8.2 0.3 copy-done
  8.5 4.3 gather_fusion.1
  12.7 3.8 gather.29
  16.6 10.4 %gather_fusion.2 = bf16[32,49152]{1,0:T(8,128)(2,1)} fusion(bf16[64,49152]{1,0:T(8,128)(2,1)} %param.10, s32[1024]{0:T(1024)S(1)} %pad_clamp_fusion), kind=kCustom, calls=%fused_computation.2 | custom fusion | bytes 6291584 | tf_op jit(solution)/shard_map/jit(_take)/gather | solution.py:69
  27.0 5.4 gather.31
  32.4 0.1 broadcast_in_dim.67
  32.5 0.1 broadcast_in_dim.71
  32.6 9.9 %multiply_convert_fusion = bf16[16,2,49152]{2,1,0:T(2,128)(2,1)} fusion(bf16[16,2,49152]{2,1,0:T(2,128)(2,1)S(1)} %gather.29, pred[16,2]{1,0:T(8,128)(4,1)S(1)} %broadcast_in_dim.67, bf16[16,2,49152]{2,1,0:T(2,128)(2,1)} %gather.31, pred[16,2]{1,0:T(8,128)(4,1)S(1)} %broadcast_in_dim.71), kind=kLoop, calls=%fused_computation.63 | loop fusion | flops 9437184 | bytes 9437248 | tf_op jit(solution)/shard_map/convert_element_type | solution.py:70
  42.6 0.0 copy-start.4
  42.6 6.6 %all-to-all-start = ((bf16[16,2,49152]{2,1,0:T(2,128)(2,1)}), bf16[16,2,49152]{2,1,0:T(2,128)(2,1)}, u32[]{:S(2)}, u32[]{:S(2)}) async-start(bf16[16,2,49152]{2,1,0:T(2,128)(2,1)} %multiply_convert_fusion), calls=%async_computation | async-start | bytes 6291456 | tf_op jit(solution)/shard_map/all_to_all | solution.py:89
  49.2 0.0 reduce-scatter.2.cloned.1.call-start
  49.3 0.0 copy-done.2
  49.3 0.7 gather_fusion.3
  50.0 0.7 gather_fusion.4
  50.7 0.0 copy-done.5
  50.7 0.0 copy-done.6
  50.8 36.0 %all-to-all-done = bf16[16,2,49152]{2,1,0:T(2,128)(2,1)} async-done(((bf16[16,2,49152]{2,1,0:T(2,128)(2,1)}), bf16[16,2,49152]{2,1,0:T(2,128)(2,1)}, u32[]{:S(2)}, u32[]{:S(2)}) %all-to-all-start) | async-done | bytes 3145760 | tf_op jit(solution)/shard_map/all_to_all | solution.py:89
  86.7 261.8 %while.14 = (s32[]{:T(128)}, f32[2,8192]{1,0:T(2,128)S(1)}, s32[4096]{0:T(1024)S(1)}, s32[4096]{0:T(1024)S(1)}, bf16[2,786432]{1,0:T(2,128)(2,1)}, /*index=5*/s32[]{:T(128)}, s32[]{:T(128)}) while((s32[]{:T(128)}, f32[2,8192]{1,0:T(2,128)S(1)}, s32[4096]{0:T(1024)S(1)}, s32[4096]{0:T(1024)S(1)}, bf16[2,786432]{1,0:T(2,128)(2,1)}, ...), condition=%wide.region_3.4_spmd.clone, body=%wide.region_0.3_spmd.clone.sunk | while | flops 6046724096 | bytes 55238740 | solution.py:92
  99.4 25.2 %dynamic-slice_reduce_fusion.2 = bf16[786432]{0:T(1024)(128)(2,1)} fusion(bf16[2,786432]{1,0:T(2,128)(2,1)} %get-tuple-element.214, s32[]{:T(128)} %get-tuple-element.203), kind=kLoop, calls=%fused_computation.10.clone.1 | loop fusion | bytes 3145732 | tf_op jit(solution)/shard_map/while/body/jit(dynamic_index_in_dim)/dynamic_slice | solution.py:92
  124.6 3.1 reshape.505
  127.7 0.8 sine_negate_fusion.2
  128.5 3.7 fusion.53
  132.2 0.1 fusion.55
  132.4 0.1 fusion.54
  132.5 9.6 %fusion.56 = f32[1,64,2,64,192]{4,3,1,2,0:T(8,128)} fusion(f32[64,64,2,192]{3,1,2,0:T(8,128)S(1)} %fusion.53, f32[64,1,2,64]{0,3,1,2:T(8,128)S(1)} %get-tuple-element.190, f32[64,1,2,64]{0,3,1,2:T(8,128)S(1)} %get-tuple-element.191), kind=kOutput, calls=%fused_computation.9.clone.1 | convolution fusion | flops 2415935488 | bytes 12648448 | tf_op jit(solution)/shard_map/while/body/eval_jaxpr/maysk,ystj->matjk/dot_general | solution.py:31
  142.2 15.4 %copy.43 = f32[1,64,2,64,192]{1,2,4,3,0:T(2,128)} copy(f32[1,64,2,64,192]{4,3,1,2,0:T(8,128)} %fusion.56) | data formatting | bytes 12582912 | tf_op jit(solution)/shard_map/while/body/eval_jaxpr/reshape | solution.py:32
  157.7 32.8 %gather_fusion = f32[4096,64,2]{1,2,0:T(2,128)} fusion(f32[64,2,12288]{0,1,2:T(2,128)} %bitcast.86, s32[4096]{0:T(1024)S(1)} %broadcast_clamp_fusion.2), kind=kCustom, calls=%fused_computation.clone.clone.1 | custom fusion | bytes 4210688 | tf_op jit(solution)/shard_map/while/body/eval_jaxpr/jit(_take)/gather | solution.py:86
  190.5 16.3 %bitcast_select_fusion.2 = f32[1,64,2,4096]{1,2,3,0:T(2,128)S(1)} fusion(f32[4096,64,2]{1,2,0:T(2,128)} %gather_fusion, pred[4096]{0:T(1024)(128)(4,1)S(1)} %compare_and_fusion.4), kind=kLoop, calls=%fused_computation.8.clone.1 | loop fusion | flops 524288 | bytes 4198400 | tf_op jit(solution)/shard_map/while/body/eval_jaxpr/jit(_take)/select_n | solution.py:86
  206.9 3.3 fusion.57
  210.2 11.2 %add_reduce_fusion.2 = (f32[4096]{0:T(1024)S(1)}, f32[4096]{0:T(1024)S(1)}) fusion(f32[1,64,4096]{1,2,0:T(8,128)S(1)} %bitcast.88, f32[1,64,4096]{1,2,0:T(8,128)S(1)} %bitcast.87, s32[4096]{0:T(1024)S(1)} %get-tuple-element.212), kind=kLoop, calls=%fused_computation.23.clone.1 | loop fusion | flops 5758976 | bytes 2146304 | tf_op jit(solution)/shard_map/while/body/eval_jaxpr/reduce_sum | solution.py:47
  221.4 0.6 copy.44
  222.1 1.4 broadcast_in_dim.93
  223.5 0.3 dynamic_update_slice.10
  223.9 25.2 %dynamic-slice_reduce_fusion.2 = bf16[786432]{0:T(1024)(128)(2,1)} fusion(bf16[2,786432]{1,0:T(2,128)(2,1)} %get-tuple-element.214, s32[]{:T(128)} %get-tuple-element.203), kind=kLoop, calls=%fused_computation.10.clone.1 | loop fusion | bytes 3145732 | tf_op jit(solution)/shard_map/while/body/jit(dynamic_index_in_dim)/dynamic_slice | solution.py:92
  249.1 3.1 reshape.505
  252.2 0.8 sine_negate_fusion.2
  253.0 3.7 fusion.53
  256.7 0.1 fusion.55
  256.9 0.1 fusion.54
  257.0 9.6 %fusion.56 = f32[1,64,2,64,192]{4,3,1,2,0:T(8,128)} fusion(f32[64,64,2,192]{3,1,2,0:T(8,128)S(1)} %fusion.53, f32[64,1,2,64]{0,3,1,2:T(8,128)S(1)} %get-tuple-element.190, f32[64,1,2,64]{0,3,1,2:T(8,128)S(1)} %get-tuple-element.191), kind=kOutput, calls=%fused_computation.9.clone.1 | convolution fusion | flops 2415935488 | bytes 12648448 | tf_op jit(solution)/shard_map/while/body/eval_jaxpr/maysk,ystj->matjk/dot_general | solution.py:31
  266.7 15.4 %copy.43 = f32[1,64,2,64,192]{1,2,4,3,0:T(2,128)} copy(f32[1,64,2,64,192]{4,3,1,2,0:T(8,128)} %fusion.56) | data formatting | bytes 12582912 | tf_op jit(solution)/shard_map/while/body/eval_jaxpr/reshape | solution.py:32
  282.1 32.8 %gather_fusion = f32[4096,64,2]{1,2,0:T(2,128)} fusion(f32[64,2,12288]{0,1,2:T(2,128)} %bitcast.86, s32[4096]{0:T(1024)S(1)} %broadcast_clamp_fusion.2), kind=kCustom, calls=%fused_computation.clone.clone.1 | custom fusion | bytes 4210688 | tf_op jit(solution)/shard_map/while/body/eval_jaxpr/jit(_take)/gather | solution.py:86
  315.0 16.3 %bitcast_select_fusion.2 = f32[1,64,2,4096]{1,2,3,0:T(2,128)S(1)} fusion(f32[4096,64,2]{1,2,0:T(2,128)} %gather_fusion, pred[4096]{0:T(1024)(128)(4,1)S(1)} %compare_and_fusion.4), kind=kLoop, calls=%fused_computation.8.clone.1 | loop fusion | flops 524288 | bytes 4198400 | tf_op jit(solution)/shard_map/while/body/eval_jaxpr/jit(_take)/select_n | solution.py:86
  331.3 3.3 fusion.57
  334.7 11.2 %add_reduce_fusion.2 = (f32[4096]{0:T(1024)S(1)}, f32[4096]{0:T(1024)S(1)}) fusion(f32[1,64,4096]{1,2,0:T(8,128)S(1)} %bitcast.88, f32[1,64,4096]{1,2,0:T(8,128)S(1)} %bitcast.87, s32[4096]{0:T(1024)S(1)} %get-tuple-element.212), kind=kLoop, calls=%fused_computation.23.clone.1 | loop fusion | flops 5758976 | bytes 2146304 | tf_op jit(solution)/shard_map/while/body/eval_jaxpr/reduce_sum | solution.py:47
  345.9 0.6 copy.44
  346.5 1.4 broadcast_in_dim.93
  348.0 0.3 dynamic_update_slice.10
  348.6 22.3 %all-gather = bf16[16,2,8192]{2,1,0:T(2,128)(2,1)S(1)} all-gather(bf16[1,2,8192]{2,1,0:T(2,128)(2,1)S(1)} %fusion.38), channel_id=1, replica_groups=mesh['pair'=16,'row'=4,'col'=4] {'row','col'}, dimensions={0}, use_global_device_ids=true | all-gather | bytes 557056 | tf_op jit(solution)/shard_map/all_gather | solution.py:94
  370.9 0.2 reshape.485
  371.1 0.4 reshape.435
  371.4 0.3 constant_dynamic-slice_fusion.1
  371.7 0.1 multiply_convert_fusion.1
  371.8 0.3 copy.31
  372.1 0.3 convert_element_type.121
  372.4 0.3 copy.39
  372.7 1.0 reshape.436
  373.6 3.8 fusion.41
  377.4 0.0 reduce-scatter.2.cloned.1.call-update
  377.4 214.5 %reduce-scatter.2.cloned.1.call-done = f32[64,1024]{1,0:T(8,128)} async-done(((f32[1024,1024]{1,0:T(8,128)}), f32[64,1024]{1,0:T(8,128)}) %reduce-scatter.2.cloned.1.call-update) | async-done | bytes 262160 | tf_op jit(solution)/shard_map/reduce_scatter | solution.py:106
  591.9 0.0 copy-done.1
  (24 shorter events, 0.3 us)
Async XLA Ops:
  6.5 1.9 copy-start
  42.6 6.7 %copy-start.2 = (f32[64]{0:T(128)S(1)}, f32[64]{0:T(128)}, u32[]{:S(2)}) copy-start(f32[64]{0:T(128)} %param.12) | copy-start | bytes 772
  42.6 7.4 %copy-start.3 = (f32[32]{0:T(128)S(1)}, f32[32]{0:T(128)}, u32[]{:S(2)}) copy-start(f32[32]{0:T(128)} %param.11) | copy-start | bytes 388
  42.6 8.1 %copy-start.5 = (s32[32]{0:T(128)S(1)}, s32[32]{0:T(128)}, u32[]{:S(2)}) copy-start(s32[32]{0:T(128)} %param.14) | copy-start | bytes 388
  42.6 8.1 %copy-start.6 = (s32[32]{0:T(128)S(1)}, s32[32]{0:T(128)}, u32[]{:S(2)}) copy-start(s32[32]{0:T(128)} %param.13) | copy-start | bytes 388
  42.6 8.2 %copy-start.4 = (s32[4096]{0:T(1024)S(1)}, s32[4096]{0:T(1024)}, u32[]{:S(2)}) copy-start(s32[4096]{0:T(1024)} %param.15) | copy-start | bytes 49156
  42.6 44.2 %all-to-all-start = ((bf16[16,2,49152]{2,1,0:T(2,128)(2,1)}), bf16[16,2,49152]{2,1,0:T(2,128)(2,1)}, u32[]{:S(2)}, u32[]{:S(2)}) async-start(bf16[16,2,49152]{2,1,0:T(2,128)(2,1)} %multiply_convert_fusion), calls=%async_computation | async-start | bytes 6291456 | tf_op jit(solution)/shard_map/all_to_all | solution.py:89
  49.2 542.7 %reduce-scatter.2.cloned.1.call-start = ((), (), s32[]{:S(2)}) async-start(), calls=%async_computation.2 | async-start | bytes 4456448 | tf_op jit(solution)/shard_map/reduce_scatter | solution.py:106
  373.6 218.3 %copy-start.1 = (bf16[32,49152]{1,0:T(8,128)(2,1)S(1)}, bf16[32,49152]{1,0:T(8,128)(2,1)}, u32[]{:S(2)}) copy-start(bf16[32,49152]{1,0:T(8,128)(2,1)} %param.9) | copy-start | bytes 9437188
Sparse Core Ops, SparseCore 0:
  377.5 214.3 reduce-scatter.1
where the time goes:
time: 607 us; the launch traced here: 599 us
  waiting for transfers between devices  251 us (41%)
  local copies, waits for them, and re-layouts  193 us (32%)
  other arithmetic  69.1 us (11%)
  matrix products  30.5 us (5%)
  blocking collectives  22.3 us (4%)
  between operations  13.8 us (2%)
  loops' own time  13 us (2%)
  starting transfers between devices  6.68 us (1%)
    reduce_scatter x1, waiting for transfers between devices, body(): lax.psum_scatter(contract_last(weighted, column_side), 'pair', scatter_di...  215 us
    gather x2, local copies, waits for them, and re-layouts, one_grid(): picked = jnp.take(spectrum, inner_ids, axis=3)  65.7 us
    dynamic_slice x2, local copies, waits for them, and re-layouts, body(): stacked = lax.map(one_grid, grids) * factor  50.4 us
    all_to_all x1, waiting for transfers between devices, body(): lax.all_to_all(grouped_rows, ('row', 'col'), split_axis=0, concat_axis=2,...  36 us
    select_n x4, other arithmetic, one_grid(): picked = jnp.take(spectrum, inner_ids, axis=3)  32.7 us
    reshape x2, local copies, waits for them, and re-layouts, yz_spectrum(): return after_y.reshape(items, planes, 2, side_y * side_z)  30.9 us
    reduce_sum x2, other arithmetic, x_finish(): jnp.sum(cosine_table * real_part + sine_table * imag_part, axis=1)  22.4 us
    all_gather x1, blocking collectives, body(): lax.all_gather(own_columns, ('row', 'col'), axis=1, tiled=True)  22.3 us
  transfers between devices with their start and end apart: 2, of which 2 were waited for; matrix products, arithmetic and copies ran while one was open for 0% of the time, Pallas kernels for 0%

commit v1 on v0

v1 whole, which is shorter than its diff:
```python
import math
import numpy as np
import jax, jax.numpy as jnp
from jax import lax
from jax.experimental import pallas as pl
from jax.experimental.pallas import tpu as pltpu
from jax.sharding import PartitionSpec as P
import ml_dtypes
BF=ml_dtypes.bfloat16
GX=64;GY=64;GZ=192;NG=4096
KZ=104

def split_hi_lo(t):
    hi=t.astype(np.float32).astype(BF); lo=(t-hi.astype(np.float64)).astype(np.float32).astype(BF)
    return hi,lo

def z_tables():
    z=np.arange(GZ); k=np.arange(97)
    ang=2*np.pi/GZ*((k[:,None]*z[None,:])%GZ)
    t=np.zeros((2,KZ,GZ)); t[0,:97]=np.cos(ang); t[1,:97]=-np.sin(ang)
    t=t.reshape(2*KZ,GZ)
    out=np.zeros((2,2*KZ,512),BF)
    hi,lo=split_hi_lo(t)
    for par,off in ((0,0),(1,64)):
        out[par,:,off:off+GZ]=hi; out[par,:,256+off:256+off+GZ]=lo
    return out

def x_tables():
    factor=1.0/math.sqrt(GX*GY*GZ)
    out=np.zeros((16,256,512),BF)
    fx=np.arange(64)
    for d in range(16):
        xs=4*d+np.arange(4)
        ang=2*np.pi/GX*((fx[:,None]*xs[None,:])%GX)
        c=np.repeat(np.cos(ang),32,axis=1)*factor; s=np.repeat(np.sin(ang),32,axis=1)*factor
        for f,sig in ((0,1.0),(1,-1.0)):
            t=np.concatenate([c,sig*s,sig*c,-s],axis=1)
            hi,lo=split_hi_lo(t)
            out[d,f*64:(f+1)*64]=hi; out[d,128+f*64:128+(f+1)*64]=lo
    return out

def fft8(v):
    def add(a,b): return (a[0]+b[0],a[1]+b[1])
    def sub(a,b): return (a[0]-b[0],a[1]-b[1])
    def mi(a): return (a[1],-a[0])
    r=np.float32(math.sqrt(0.5))
    def fft4(x0,x1,x2,x3):
        a=add(x0,x2); b=sub(x0,x2); c=add(x1,x3); d=mi(sub(x1,x3))
        return add(a,c),add(b,d),sub(a,c),sub(b,d)
    e=fft4(v[0],v[2],v[4],v[6]); o=fft4(v[1],v[3],v[5],v[7])
    o1=((o[1][0]+o[1][1])*r,(o[1][1]-o[1][0])*r)
    o2=mi(o[2])
    o3=((o[3][1]-o[3][0])*r,-(o[3][0]+o[3][1])*r)
    os=(o[0],o1,o2,o3)
    return [add(e[k],os[k]) for k in range(4)]+[sub(e[k],os[k]) for k in range(4)]

def transform_kernel(val_s, con_s, row_s, dev_s, pv, pc, kcode, ztab, xtab, out, rho, Z, Z2, GA, GB):
    step=pl.program_id(0)
    sub=lax.broadcasted_iota(jnp.int32,(64,96),0); lane=lax.broadcasted_iota(jnp.int32,(64,96),1)
    want=jnp.zeros((64,96),jnp.int32)
    for p in range(32):
        want=jnp.where(sub==p, val_s[p], want)
        want=jnp.where(sub==32+p, con_s[p]+32, want)
    sel=(want==lane).astype(jnp.bfloat16)
    CH=512; NU=24
    def rho_body(i,_):
        for u in range(NU):
            o=pl.multiple_of(i*(CH*NU)+u*CH,CH)
            src=jnp.concatenate([pv[:,pl.ds(o,CH)],pc[:,pl.ds(o,CH)]],axis=0)
            res=jnp.dot(sel,src,preferred_element_type=jnp.float32)
            rho[step,:,pl.ds(o,CH)]=(res[:32]*res[32:]).astype(jnp.bfloat16)
        return 0
    lax.fori_loop(0,12288//(CH*NU),rho_body,0)

    @pl.when(step==3)
    def _():
        for b in range(8):
            wt=ztab[b%2]
            for ah in range(4):
                parts=[]
                for a in (2*ah,2*ah+1):
                    yp=4*a+b//2; o=384*yp+128*(b%2)
                    for x in range(4):
                        parts.append(rho[x,:,o:o+256])
                B=jnp.concatenate(parts,axis=0)
                B=jnp.concatenate([B,B],axis=1)
                res=lax.dot_general(wt,B,(((1,),(1,)),((),())),preferred_element_type=jnp.float32)
                Z[pl.ds((8*(2*ah)+b)*2*KZ,2*KZ),:]=res[:,:128]
                Z[pl.ds((8*(2*ah+1)+b)*2*KZ,2*KZ),:]=res[:,128:]
        tw=[[np.exp(-2j*np.pi*b*k/64) for k in range(8)] for b in range(8)]
        def pass1(j,_):
            r0=pl.multiple_of(j*8,8)
            for b in range(8):
                v=[(Z[pl.ds((8*a+b)*2*KZ+r0,8),:],Z[pl.ds((8*a+b)*2*KZ+KZ+r0,8),:]) for a in range(8)]
                w=fft8(v)
                for k in range(8):
                    re,im=w[k]
                    if b and k:
                        c=np.float32(tw[b][k].real); s=np.float32(tw[b][k].imag)
                        re,im=re*c-im*s, re*s+im*c
                    Z[pl.ds((8*k+b)*2*KZ+r0,8),:]=re; Z[pl.ds((8*k+b)*2*KZ+KZ+r0,8),:]=im
            return 0
        lax.fori_loop(0,KZ//8,pass1,0)
        def pass2(j,_):
            r0=pl.multiple_of(j*8,8)
            for k1 in range(8):
                v=[(Z[pl.ds((8*k1+b)*2*KZ+r0,8),:],Z[pl.ds((8*k1+b)*2*KZ+KZ+r0,8),:]) for b in range(8)]
                w=fft8(v)
                for k in range(8):
                    re,im=w[k]
                    base=(8*k1+k)*2*KZ+2*r0
                    Z2[pl.ds(base,8,stride=2),:]=re; Z2[pl.ds(base+1,8,stride=2),:]=im
            return 0
        lax.fori_loop(0,KZ//8,pass2,0)
        ksub=lax.broadcasted_iota(jnp.int32,(128,256),0)
        ln=lax.broadcasted_iota(jnp.int32,(128,128),1)
        lnb=lax.broadcasted_iota(jnp.int32,(256,128),1)
        def gather(t,G):
            base=t*256
            for j in range(256):
                rr=pl.multiple_of(row_s[base+j],2)
                G[pl.ds(2*j,2),:]=Z2[pl.ds(rr,2),:]
        def phase(t,G):
            base=t*256
            code=kcode[:,pl.ds(pl.multiple_of(base,256),256)]
            oh=(ksub==code).astype(jnp.bfloat16)
            oh=jnp.concatenate([oh,oh],axis=0)
            co=lax.dot_general(oh,xtab[0],(((0,),(0,)),((),())),preferred_element_type=jnp.float32)
            R=G[pl.ds(0,256,stride=2),:]; I=G[pl.ds(1,256,stride=2),:]
            re=co[:,:128]*R+co[:,128:256]*I
            im=co[:,256:384]*I+co[:,384:]*R
            t1=re+pltpu.roll(re,64,1); u1=im+pltpu.roll(im,64,1)
            w=jnp.where(lnb<64,t1,u1)
            w0=w[:128]; w1=w[128:]
            v0=w0+pltpu.roll(w0,96,1)
            v1=w1+pltpu.roll(w1,32,1)
            out[(t%4)*4+t//4]=jnp.where((ln%64)<32,v0,v1).astype(jnp.bfloat16)
        gather(0,GA)
        def pairs(u,_):
            t=2*u
            gather(t+1,GB); phase(t,GA)
            gather(jnp.minimum(t+2,15),GA); phase(t+1,GB)
            return 0
        lax.fori_loop(0,8,pairs,0)

def prep(gmap):
    fz=gmap%GZ; q=gmap//GZ; fy=q%GY; fx=q//GY
    flag=(fz>96).astype(jnp.int32)
    fz2=jnp.where(fz>96,GZ-fz,fz); fy2=jnp.where(fz>96,(GY-fy)%GY,fy)
    loc=8*(fy2%8)+fy2//8
    rows=loc*(2*KZ)+2*fz2
    return rows, (flag*64+fx)

def kernel1(val_idx,con_idx,rows,code,dev,pv,pc):
    return pl.pallas_call(
        transform_kernel,
        grid_spec=pltpu.PrefetchScalarGridSpec(
            num_scalar_prefetch=4, grid=(4,),
            in_specs=[pl.BlockSpec((32,12288),lambda i,*_:(0,i)),
                      pl.BlockSpec((64,12288),lambda i,*_:(0,i)),
                      pl.BlockSpec((1,NG),lambda i,*_:(0,0)),
                      pl.BlockSpec((2,2*KZ,512),lambda i,*_:(0,0,0)),
                      pl.BlockSpec((1,256,512),lambda i,a,b,c,d:(d[0],0,0))],
            out_specs=pl.BlockSpec((16,128,128),lambda i,*_:(0,0,0)),
            scratch_shapes=[pltpu.VMEM((4,32,12288),jnp.bfloat16),
                            pltpu.VMEM((64*2*KZ,128),jnp.float32),
                            pltpu.VMEM((64*2*KZ,128),jnp.float32),pltpu.VMEM((512,128),jnp.float32),pltpu.VMEM((512,128),jnp.float32)]),
        out_shape=jax.ShapeDtypeStruct((16,128,128),jnp.bfloat16),
        compiler_params=pltpu.CompilerParams(vmem_limit_bytes=48*2**20, dimension_semantics=("arbitrary",)),
        name="partial_transform",
    )(val_idx,con_idx,rows,dev,pv,pc,code.reshape(1,NG),jnp.asarray(z_tables()),jnp.asarray(x_tables()))


def sum_kernel(val_s,con_s,ev_s,ec_s,recv,out):
    acc=recv[0].astype(jnp.float32)
    for i in range(1,16):
        acc=acc+recv[i].astype(jnp.float32)
    pid=lax.broadcasted_iota(jnp.int32,(16,128),1)%32
    ev=jnp.zeros((16,128),jnp.float32); ec=jnp.ones((16,128),jnp.float32)
    for p in range(32):
        ev=jnp.where(pid==p,ev_s[val_s[p]],ev)
        ec=jnp.where(pid==p,ec_s[con_s[p]],ec)
    w=-2.0/(math.sqrt(512)*(ec-ev))
    hi=w.astype(jnp.bfloat16).astype(jnp.float32)
    mid=(w-hi).astype(jnp.bfloat16).astype(jnp.float32)
    lo=w-hi-mid
    row=lax.broadcasted_iota(jnp.int32,(16,128),0)
    wr=jnp.where(row==0,hi,jnp.where(row==1,mid,lo)).astype(jnp.bfloat16)
    full=jnp.concatenate([acc.astype(jnp.bfloat16),wr],axis=0)
    for i in range(16):
        out[i]=full

def tile_kernel(t,rw,out,lhs):
    half=lax.axis_index("row")//2
    ln=lax.broadcasted_iota(jnp.int32,(64,128),1)
    first=(ln%64)<32
    for g in range(16):
        w=t[0,g,128:144,:].astype(jnp.float32)
        w=w[0:1]+w[1:2]+w[2:3]
        d=rw[g].astype(jnp.float32)
        d=jnp.where(half==1,pltpu.roll(d,96,1),d)
        d=jnp.where(first,d*w,0.0)
        lhs[g,0:64,:]=d.astype(jnp.bfloat16)
        lhs[g,64:128,:]=pltpu.roll(d,32,1).astype(jnp.bfloat16)
    for r in range(4):
        acc=jnp.zeros((128,128),jnp.float32)
        for g in range(16):
            acc=acc+lax.dot_general(lhs[g],t[r,g,0:128,:],(((1,),(1,)),((),())),preferred_element_type=jnp.float32)
        out[:,256*r:256*r+128]=acc[:64]
        out[:,256*r+128:256*r+256]=acc[64:]

SMEM=pl.BlockSpec(memory_space=pltpu.SMEM)
VM=pl.BlockSpec(memory_space=pltpu.VMEM)

def body(psi_val, psi_con, e_val, e_con, val_idx, con_idx, gmap):
    pair=lax.axis_index("pair"); row=lax.axis_index("row"); col=lax.axis_index("col")
    rows,code=prep(gmap)
    part=kernel1(val_idx,con_idx,rows,code,(row*4+col).reshape(1),psi_val,psi_con)
    recv=lax.all_to_all(part,("row","col"),split_axis=0,concat_axis=0,tiled=True)
    payload=pl.pallas_call(sum_kernel,in_specs=[SMEM]*4+[VM],out_specs=VM,
        out_shape=jax.ShapeDtypeStruct((16,144,128),jnp.bfloat16),name="sum_parts")(val_idx,con_idx,e_val,e_con,recv)
    groups=lax.all_to_all(payload,"pair",split_axis=0,concat_axis=0,tiled=True)
    perm=[]
    for p in range(16):
        for r in range(4):
            for c in range(4):
                perm.append(((r*4+c)*16+(p%4)*4+p//4, p*16+r*4+c))
    piece=lax.dynamic_slice_in_dim(groups,((pair//4)%2)*64,64,1)
    rowpart=lax.ppermute(piece,("pair","row","col"),perm)
    full=lax.all_gather(groups,"row",axis=0)
    return pl.pallas_call(tile_kernel,in_specs=[VM,VM],out_specs=VM,
        out_shape=jax.ShapeDtypeStruct((64,1024),jnp.float32),
        scratch_shapes=[pltpu.VMEM((16,128,128),jnp.bfloat16)],
        compiler_params=pltpu.CompilerParams(vmem_limit_bytes=16*2**20),
        name="tile")(full,rowpart)

def solution(mesh):
    return jax.shard_map(
        body,
        mesh=mesh,
        in_specs=(
            P(None, ("row", "col")),
            P(None, ("row", "col")),
            P(),
            P(),
            P("pair"),
            P("pair"),
            P(),
        ),
        out_specs=P(("pair", "row"), "col"),
        check_vma=False,
    )
```

time: 607 us -> 126 us (0.21); the launches traced: 599 us -> 125 us
  waiting for transfers between devices: 251 us -> 32.2 us
  local copies, waits for them, and re-layouts: 193 us -> 6.84 us
  other arithmetic: 69.1 us -> 0.79 us
  matrix products: 30.5 us -> 0 us
  blocking collectives: 22.3 us -> 46.1 us
  Pallas kernels: 0 us -> 21.7 us
  loops' own time: 13 us -> 0 us
    reduce_scatter x1 -> x0, waiting for transfers between devices: 215 us -> none  [body(): lax.psum_scatter(contract_last(weighted, column_side), 'pair', scatter_di...]
    gather x8 -> x0, local copies, waits for them, and re-layouts: 91.1 us -> none  [the longest x2 65.7 us: one_grid(): picked = jnp.take(spectrum, inner_ids, axis=3)]
    dynamic_slice x3 -> x1, local copies, waits for them, and re-layouts: 50.7 us -> 0.98 us  [body(): piece = lax.dynamic_slice_in_dim(groups, pair // 4 % 2 * 64, 64, 1)]
    all_to_all x0 -> x2, blocking collectives: none -> 46.1 us  [the longest x1 31.9 us: body(): lax.all_to_all(payload, 'pair', split_axis=0, concat_axis=0, tiled=True)]
    all_to_all x1 -> x0, waiting for transfers between devices: 36 us -> none  [body(): lax.all_to_all(grouped_rows, ('row', 'col'), split_axis=0, concat_axis=2,...]
    select_n x6 -> x0, other arithmetic: 33.5 us -> none  [the longest x4 32.7 us: one_grid(): picked = jnp.take(spectrum, inner_ids, axis=3)]
    reshape x4 -> x0, local copies, waits for them, and re-layouts: 32.2 us -> none  [the longest x2 30.9 us: yz_spectrum(): return after_y.reshape(items, planes, 2, side_y * side_z)]
    dot_general x5 -> x0, matrix products: 30.5 us -> none  [the longest x2 19.3 us: yz_spectrum(): after_y = jnp.einsum('maysk,ystj->matjk', after_z, table_y, precision=high)]
  transfers between devices with their start and end apart: 2 -> 2, of which waited for: 2 -> 2; matrix products, arithmetic and copies ran while one was open for 0% -> 1% of each run, Pallas kernels for 0% -> 0%
where the time goes in v1:
time: 126 us; the launch traced here: 125 us
  blocking collectives  46.1 us (37%)
  waiting for transfers between devices  32.2 us (26%)
  Pallas kernels  21.7 us (17%)
  between operations  13.5 us (11%)
  local copies, waits for them, and re-layouts  6.84 us (5%)
  starting transfers between devices  3.78 us (3%)
    all_to_all x1, blocking collectives, body(): lax.all_to_all(payload, 'pair', split_axis=0, concat_axis=0, tiled=True)  31.9 us
    all_gather x1, waiting for transfers between devices, body(): full = lax.all_gather(groups, 'row', axis=0)  22.6 us
    pallas_call x1, Pallas kernels, kernel1(): pl.pallas_call(transform_kernel, grid_spec=pltpu.PrefetchScalarGridSpec(n...  17.2 us
    all_to_all x1, blocking collectives, body(): lax.all_to_all(part, ('row', 'col'), split_axis=0, concat_axis=0, tiled=T...  14.3 us
    ppermute x1, waiting for transfers between devices, body(): rowpart = lax.ppermute(piece, ('pair', 'row', 'col'), perm)  9.54 us
    unnamed x10, local copies, waits for them, and re-layouts  5.87 us
    ppermute x1, starting transfers between devices, body(): rowpart = lax.ppermute(piece, ('pair', 'row', 'col'), perm)  3.78 us
    pallas_call x1, Pallas kernels, body(): pl.pallas_call(tile_kernel, in_specs=[VM, VM], out_specs=VM, out_shape=ja...  2.54 us
  transfers between devices with their start and end apart: 2, of which 2 were waited for; matrix products, arithmetic and copies ran while one was open for 1% of the time, Pallas kernels for 0%

profile of v1, /device:TPU:2, one launch (start us, length us, event | category | flops | bytes accessed | tf_op | source)
XLA Modules:
  0.0 124.9 jit_solution(2370204913300220865)
XLA Ops:
  6.5 0.0 all-gather.3.cloned.1.call-start
  6.5 0.8 fusion.7
  7.3 0.0 copy-start
  7.3 1.9 %copy-done = bf16[32,49152]{1,0:T(8,128)(2,1)S(1)} copy-done((bf16[32,49152]{1,0:T(8,128)(2,1)S(1)}, bf16[32,49152]{1,0:T(8,128)(2,1)}, u32[]{:S(2)}) %copy-start) | copy-done | bytes 3145752
  9.2 0.0 copy-start.2
  9.2 1.0 copy-done.2
  10.2 0.0 copy-start.3
  10.2 0.7 copy-done.3
  10.9 0.0 copy-start.4
  10.9 0.7 copy-done.4
  11.5 17.2 %partial_transform.1 = bf16[16,128,128]{2,1,0:T(8,128)(2,1)S(1)} custom-call(s32[32]{0:T(128)S(1)} %copy-done.3, s32[32]{0:T(128)S(1)} %copy-done.4, s32[4096]{0:T(1024)S(1)} %get-tuple-element.6.row_s, s32[1]{0:T(128)} %bitcast.dev_s, bf16[32,49152]{1,0:T(8,128)(2,1)S(1)} %copy-done, bf16[64,49152]{1,0:T(8,128)(2,1)} %pc.1, s32[1,4096]{1,0:T(1,128)S(1)} %bitcast.4, ...), custom_call_target="tpu_custom_call" | custom-call | tf_op jit(solution)/shard_map/partial_transform/pallas_call | solution.py:155
  28.7 14.3 %all_to_all.10.recv = bf16[16,128,128]{2,1,0:T(8,128)(2,1)} all-to-all(bf16[16,128,128]{2,1,0:T(8,128)(2,1)S(1)} %partial_transform.1), channel_id=1, replica_groups=mesh['pair'=16,'row'=4,'col'=4] {'row','col'}, dimensions={0} | all-to-all | bytes 1048576 | tf_op jit(solution)/shard_map/all_to_all | solution.py:219
  43.0 2.0 %sum_parts.1 = bf16[16,144,128]{2,1,0:T(8,128)(2,1)} custom-call(s32[32]{0:T(128)} %val_s.3, s32[32]{0:T(128)} %con_s.3, f32[32]{0:T(128)} %ev_s.1, f32[64]{0:T(128)} %ec_s.1, bf16[16,128,128]{2,1,0:T(8,128)(2,1)} %all_to_all.10.recv), custom_call_target="tpu_custom_call" | custom-call | tf_op jit(solution)/shard_map/sum_parts/pallas_call | solution.py:220
  45.0 31.9 %all_to_all.11 = bf16[16,144,128]{2,1,0:T(8,128)(2,1)} all-to-all(bf16[16,144,128]{2,1,0:T(8,128)(2,1)} %sum_parts.1), channel_id=1, replica_groups=mesh['pair'=16,'row'=4,'col'=4] {'pair'}, dimensions={0} | all-to-all | bytes 1179648 | tf_op jit(solution)/shard_map/all_to_all | solution.py:222
  76.8 0.0 all-gather.3.cloned.1.call-update
  76.9 1.0 constant_dynamic-slice_fusion
  77.9 3.8 %collective-permute-start = (bf16[16,64,128]{2,1,0:T(8,128)(2,1)S(1)}, bf16[16,64,128]{2,1,0:T(8,128)(2,1)S(1)}, u32[]{:S(2)}, u32[]{:S(2)}) collective-permute-start(bf16[16,64,128]{2,1,0:T(8,128)(2,1)S(1)} %constant_dynamic-slice_fusion), channel_id=1, source_target_pairs={{0,0},{16,1},{32,2},{48,3},{64,4},{80,5},{96,6},{112,7},{128,8},{1... | collective-permute-start | bytes 786440 | tf_op jit(solution)/shard_map/ppermute | solution.py:229
  81.7 9.5 %collective-permute-done.rw = bf16[16,64,128]{2,1,0:T(8,128)(2,1)S(1)} collective-permute-done((bf16[16,64,128]{2,1,0:T(8,128)(2,1)S(1)}, bf16[16,64,128]{2,1,0:T(8,128)(2,1)S(1)}, u32[]{:S(2)}, u32[]{:S(2)}) %collective-permute-start) | collective-permute-done | bytes 262176 | tf_op jit(solution)/shard_map/ppermute | solution.py:229
  91.2 22.6 %all-gather.3.cloned.1.call-done = bf16[64,144,128]{2,1,0:T(8,128)(2,1)} async-done(((bf16[16,144,128]{2,1,0:T(8,128)(2,1)}), bf16[64,144,128]{2,1,0:T(8,128)(2,1)}) %all-gather.3.cloned.1.call-update) | async-done | bytes 2359312 | tf_op jit(solution)/shard_map/all_gather | solution.py:230
  113.8 0.0 copy-start.1
  113.8 1.7 %copy-done.1 = bf16[64,144,128]{2,1,0:T(8,128)(2,1)S(1)} copy-done((bf16[64,144,128]{2,1,0:T(8,128)(2,1)S(1)}, bf16[64,144,128]{2,1,0:T(8,128)(2,1)}, u32[]{:S(2)}) %copy-start.1) | copy-done | bytes 2359320
  115.5 2.5 %tile.1 = f32[64,1024]{1,0:T(8,128)} custom-call(bf16[4,16,144,128]{3,2,1,0:T(8,128)(2,1)S(1)} %bitcast.3, bf16[16,64,128]{2,1,0:T(8,128)(2,1)S(1)} %collective-permute-done.rw), custom_call_target="tpu_custom_call" | custom-call | tf_op jit(solution)/shard_map/tile/pallas_call | solution.py:231
Async XLA Ops:
  6.5 107.3 %all-gather.3.cloned.1.call-start = ((), (), s32[]{:S(2)}) async-start(), calls=%async_computation.2 | async-start | bytes 2949120 | tf_op jit(solution)/shard_map/all_gather | solution.py:230
  7.3 1.9 %copy-start = (bf16[32,49152]{1,0:T(8,128)(2,1)S(1)}, bf16[32,49152]{1,0:T(8,128)(2,1)}, u32[]{:S(2)}) copy-start(bf16[32,49152]{1,0:T(8,128)(2,1)} %pv.1) | copy-start | bytes 9437188
  9.2 1.0 copy-start.2
  10.2 0.7 copy-start.3
  10.9 0.7 copy-start.4
  77.9 13.3 %collective-permute-start = (bf16[16,64,128]{2,1,0:T(8,128)(2,1)S(1)}, bf16[16,64,128]{2,1,0:T(8,128)(2,1)S(1)}, u32[]{:S(2)}, u32[]{:S(2)}) collective-permute-start(bf16[16,64,128]{2,1,0:T(8,128)(2,1)S(1)} %constant_dynamic-slice_fusion), channel_id=1, source_target_pairs={{0,0},{16,1},{32,2},{48,3},{64,4},{80,5},{96,6},{112,7},{128,8},{1... | collective-permute-start | bytes 786440 | tf_op jit(solution)/shard_map/ppermute | solution.py:229
  113.8 1.7 %copy-start.1 = (bf16[64,144,128]{2,1,0:T(8,128)(2,1)S(1)}, bf16[64,144,128]{2,1,0:T(8,128)(2,1)}, u32[]{:S(2)}) copy-start(bf16[64,144,128]{2,1,0:T(8,128)(2,1)} %all-gather.3.cloned.1.call-done) | copy-start | bytes 7077892
Sparse Core Ops, SparseCore 0:
  77.0 36.7 all-gather.2

commit v2 on v1

--- a/solution.py
+++ b/solution.py
@@ -54,8 +54,13 @@
     os=(o[0],o1,o2,o3)
     return [add(e[k],os[k]) for k in range(4)]+[sub(e[k],os[k]) for k in range(4)]
 
-def transform_kernel(val_s, con_s, row_s, dev_s, pv, pc, kcode, ztab, xtab, out, rho, Z, Z2, GA, GB):
+def transform_kernel(val_s, con_s, row_s, pv, pc, kcode, ztab, xtabs, out, rho, Z, Z2, GA, GB, xtab, xsem):
     step=pl.program_id(0)
+    place=lax.axis_index("row")*4+lax.axis_index("col")
+    fetch=pltpu.make_async_copy(xtabs.at[place],xtab,xsem)
+    @pl.when(step==0)
+    def _():
+        fetch.start()
     sub=lax.broadcasted_iota(jnp.int32,(64,96),0); lane=lax.broadcasted_iota(jnp.int32,(64,96),1)
     want=jnp.zeros((64,96),jnp.int32)
     for p in range(32):
@@ -74,6 +79,7 @@
 
     @pl.when(step==3)
     def _():
+        fetch.wait()
         for b in range(8):
             wt=ztab[b%2]
             for ah in range(4):
@@ -125,7 +131,7 @@
             code=kcode[:,pl.ds(pl.multiple_of(base,256),256)]
             oh=(ksub==code).astype(jnp.bfloat16)
             oh=jnp.concatenate([oh,oh],axis=0)
-            co=lax.dot_general(oh,xtab[0],(((0,),(0,)),((),())),preferred_element_type=jnp.float32)
+            co=lax.dot_general(oh,xtab[...],(((0,),(0,)),((),())),preferred_element_type=jnp.float32)
             R=G[pl.ds(0,256,stride=2),:]; I=G[pl.ds(1,256,stride=2),:]
             re=co[:,:128]*R+co[:,128:256]*I
             im=co[:,256:384]*I+co[:,384:]*R
@@ -134,7 +140,14 @@
             w0=w[:128]; w1=w[128:]
             v0=w0+pltpu.roll(w0,96,1)
             v1=w1+pltpu.roll(w1,32,1)
-            out[(t%4)*4+t//4]=jnp.where((ln%64)<32,v0,v1).astype(jnp.bfloat16)
+            o=jnp.where((ln%64)<32,v0,v1).T
+            c=t//4
+            for h in range(2):
+                at=pl.multiple_of((t%4)*256+h*128,128)
+                for r in range(4):
+                    lo=h*32+r*8
+                    both=jnp.concatenate([o[lo:lo+8],o[64+lo:64+lo+8]],axis=0)
+                    out[r*4+c,:,pl.ds(at,128)]=both.astype(jnp.bfloat16)
         gather(0,GA)
         def pairs(u,_):
             t=2*u
@@ -151,88 +164,82 @@
     rows=loc*(2*KZ)+2*fz2
     return rows, (flag*64+fx)
 
-def kernel1(val_idx,con_idx,rows,code,dev,pv,pc):
+def kernel1(val_idx,con_idx,rows,code,pv,pc):
+    smem=pl.BlockSpec(memory_space=pltpu.SMEM)
     return pl.pallas_call(
         transform_kernel,
-        grid_spec=pltpu.PrefetchScalarGridSpec(
-            num_scalar_prefetch=4, grid=(4,),
-            in_specs=[pl.BlockSpec((32,12288),lambda i,*_:(0,i)),
-                      pl.BlockSpec((64,12288),lambda i,*_:(0,i)),
-                      pl.BlockSpec((1,NG),lambda i,*_:(0,0)),
-                      pl.BlockSpec((2,2*KZ,512),lambda i,*_:(0,0,0)),
-                      pl.BlockSpec((1,256,512),lambda i,a,b,c,d:(d[0],0,0))],
-            out_specs=pl.BlockSpec((16,128,128),lambda i,*_:(0,0,0)),
-            scratch_shapes=[pltpu.VMEM((4,32,12288),jnp.bfloat16),
-                            pltpu.VMEM((64*2*KZ,128),jnp.float32),
-                            pltpu.VMEM((64*2*KZ,128),jnp.float32),pltpu.VMEM((512,128),jnp.float32),pltpu.VMEM((512,128),jnp.float32)]),
-        out_shape=jax.ShapeDtypeStruct((16,128,128),jnp.bfloat16),
-        compiler_params=pltpu.CompilerParams(vmem_limit_bytes=48*2**20, dimension_semantics=("arbitrary",)),
+        grid=(4,),
+        in_specs=[smem,smem,smem,
+                  pl.BlockSpec((32,12288),lambda i:(0,i)),
+                  pl.BlockSpec((64,12288),lambda i:(0,i)),
+                  pl.BlockSpec((1,NG),lambda i:(0,0)),
+                  pl.BlockSpec((2,2*KZ,512),lambda i:(0,0,0)),
+                  pl.BlockSpec(memory_space=pl.ANY)],
+        out_specs=pl.BlockSpec((16,16,1024),lambda i:(0,0,0)),
+        scratch_shapes=[pltpu.VMEM((4,32,12288),jnp.bfloat16),
+                        pltpu.VMEM((64*2*KZ,128),jnp.float32),
+                        pltpu.VMEM((64*2*KZ,128),jnp.float32),
+                        pltpu.VMEM((512,128),jnp.float32),
+                        pltpu.VMEM((512,128),jnp.float32),
+                        pltpu.VMEM((256,512),jnp.bfloat16),
+                        pltpu.SemaphoreType.DMA],
+        out_shape=jax.ShapeDtypeStruct((16,16,1024),jnp.bfloat16),
+        compiler_params=pltpu.CompilerParams(vmem_limit_bytes=60*2**20, dimension_semantics=("arbitrary",)),
         name="partial_transform",
-    )(val_idx,con_idx,rows,dev,pv,pc,code.reshape(1,NG),jnp.asarray(z_tables()),jnp.asarray(x_tables()))
-
-
-def sum_kernel(val_s,con_s,ev_s,ec_s,recv,out):
-    acc=recv[0].astype(jnp.float32)
+    )(val_idx,con_idx,rows,pv,pc,code.reshape(1,NG),jnp.asarray(z_tables()),jnp.asarray(x_tables()))
+
+def sum_kernel(parts,out):
+    acc=parts[0].astype(jnp.float32)
     for i in range(1,16):
-        acc=acc+recv[i].astype(jnp.float32)
-    pid=lax.broadcasted_iota(jnp.int32,(16,128),1)%32
-    ev=jnp.zeros((16,128),jnp.float32); ec=jnp.ones((16,128),jnp.float32)
-    for p in range(32):
-        ev=jnp.where(pid==p,ev_s[val_s[p]],ev)
-        ec=jnp.where(pid==p,ec_s[con_s[p]],ec)
+        acc=acc+parts[i].astype(jnp.float32)
+    out[...]=acc.astype(jnp.bfloat16)
+
+def payload_kernel(val_s,con_s,ev_s,ec_s,own,every,out):
+    first=lax.axis_index("row")*8
+    pid=lax.broadcasted_iota(jnp.int32,(16,256),0)%8
+    ev=jnp.zeros((16,256),jnp.float32); ec=jnp.ones((16,256),jnp.float32)
+    for p in range(8):
+        ev=jnp.where(pid==p,ev_s[val_s[first+p]],ev)
+        ec=jnp.where(pid==p,ec_s[con_s[first+p]],ec)
     w=-2.0/(math.sqrt(512)*(ec-ev))
-    hi=w.astype(jnp.bfloat16).astype(jnp.float32)
-    mid=(w-hi).astype(jnp.bfloat16).astype(jnp.float32)
-    lo=w-hi-mid
-    row=lax.broadcasted_iota(jnp.int32,(16,128),0)
-    wr=jnp.where(row==0,hi,jnp.where(row==1,mid,lo)).astype(jnp.bfloat16)
-    full=jnp.concatenate([acc.astype(jnp.bfloat16),wr],axis=0)
-    for i in range(16):
-        out[i]=full
-
-def tile_kernel(t,rw,out,lhs):
-    half=lax.axis_index("row")//2
-    ln=lax.broadcasted_iota(jnp.int32,(64,128),1)
-    first=(ln%64)<32
-    for g in range(16):
-        w=t[0,g,128:144,:].astype(jnp.float32)
-        w=w[0:1]+w[1:2]+w[2:3]
-        d=rw[g].astype(jnp.float32)
-        d=jnp.where(half==1,pltpu.roll(d,96,1),d)
-        d=jnp.where(first,d*w,0.0)
-        lhs[g,0:64,:]=d.astype(jnp.bfloat16)
-        lhs[g,64:128,:]=pltpu.roll(d,32,1).astype(jnp.bfloat16)
-    for r in range(4):
-        acc=jnp.zeros((128,128),jnp.float32)
-        for g in range(16):
-            acc=acc+lax.dot_general(lhs[g],t[r,g,0:128,:],(((1,),(1,)),((),())),preferred_element_type=jnp.float32)
-        out[:,256*r:256*r+128]=acc[:64]
-        out[:,256*r+128:256*r+256]=acc[64:]
+    mine=own[...]
+    for p in range(16):
+        out[p,:,0:1024]=mine
+        rows=every[p//4,:,256*(p%4):256*(p%4)+256].astype(jnp.float32)
+        out[p,:,1024:1280]=(rows*w).astype(jnp.bfloat16)
+
+def tile_kernel(t,out):
+    left=t[:,1024:1280].astype(jnp.float32).T.astype(jnp.bfloat16)
+    for n in range(4):
+        part=jnp.dot(left,t[:,256*n:256*n+256],preferred_element_type=jnp.float32)
+        for r in range(4):
+            out[r,:,256*n:256*n+256]=part[64*r:64*r+64].astype(out.dtype)
+
+def final_kernel(parts,out):
+    acc=parts[0].astype(jnp.float32)
+    for i in range(1,4):
+        acc=acc+parts[i].astype(jnp.float32)
+    out[...]=acc
 
 SMEM=pl.BlockSpec(memory_space=pltpu.SMEM)
 VM=pl.BlockSpec(memory_space=pltpu.VMEM)
+SEND=jnp.bfloat16
 
 def body(psi_val, psi_con, e_val, e_con, val_idx, con_idx, gmap):
-    pair=lax.axis_index("pair"); row=lax.axis_index("row"); col=lax.axis_index("col")
     rows,code=prep(gmap)
-    part=kernel1(val_idx,con_idx,rows,code,(row*4+col).reshape(1),psi_val,psi_con)
+    part=kernel1(val_idx,con_idx,rows,code,psi_val,psi_con)
     recv=lax.all_to_all(part,("row","col"),split_axis=0,concat_axis=0,tiled=True)
-    payload=pl.pallas_call(sum_kernel,in_specs=[SMEM]*4+[VM],out_specs=VM,
-        out_shape=jax.ShapeDtypeStruct((16,144,128),jnp.bfloat16),name="sum_parts")(val_idx,con_idx,e_val,e_con,recv)
+    own=pl.pallas_call(sum_kernel,in_specs=[VM],out_specs=VM,
+        out_shape=jax.ShapeDtypeStruct((16,1024),jnp.bfloat16),name="sum_parts")(recv)
+    every=lax.all_gather(own,"col",axis=0)
+    payload=pl.pallas_call(payload_kernel,in_specs=[SMEM]*4+[VM]*2,out_specs=VM,
+        out_shape=jax.ShapeDtypeStruct((16,16,1280),jnp.bfloat16),name="payload")(val_idx,con_idx,e_val,e_con,own,every)
     groups=lax.all_to_all(payload,"pair",split_axis=0,concat_axis=0,tiled=True)
-    perm=[]
-    for p in range(16):
-        for r in range(4):
-            for c in range(4):
-                perm.append(((r*4+c)*16+(p%4)*4+p//4, p*16+r*4+c))
-    piece=lax.dynamic_slice_in_dim(groups,((pair//4)%2)*64,64,1)
-    rowpart=lax.ppermute(piece,("pair","row","col"),perm)
-    full=lax.all_gather(groups,"row",axis=0)
-    return pl.pallas_call(tile_kernel,in_specs=[VM,VM],out_specs=VM,
-        out_shape=jax.ShapeDtypeStruct((64,1024),jnp.float32),
-        scratch_shapes=[pltpu.VMEM((16,128,128),jnp.bfloat16)],
-        compiler_params=pltpu.CompilerParams(vmem_limit_bytes=16*2**20),
-        name="tile")(full,rowpart)
+    tiles=pl.pallas_call(tile_kernel,in_specs=[VM],out_specs=VM,
+        out_shape=jax.ShapeDtypeStruct((4,64,1024),SEND),name="tile")(groups.reshape(256,1280))
+    tiles=lax.all_to_all(tiles,"row",split_axis=0,concat_axis=0,tiled=True)
+    return pl.pallas_call(final_kernel,in_specs=[VM],out_specs=VM,
+        out_shape=jax.ShapeDtypeStruct((64,1024),jnp.float32),name="total")(tiles)
 
 def solution(mesh):
     return jax.shard_map(

time: 126 us -> 94.3 us (0.75)
  waiting for transfers between devices: 32.2 us -> 0 us
  blocking collectives: 46.1 us -> 66.4 us
  between operations: 13.5 us -> 0.01 us
  local copies, waits for them, and re-layouts: 6.84 us -> 0 us
  starting transfers between devices: 3.78 us -> 0 us
  Pallas kernels: 21.7 us -> 25.3 us
    all_gather x1 -> x0, waiting for transfers between devices: 22.6 us -> none  [body(): full = lax.all_gather(groups, 'row', axis=0)]
    all_to_all x0 -> x1, blocking collectives: none -> 13.2 us  [body(): lax.all_to_all(tiles, 'row', split_axis=0, concat_axis=0, tiled=True)]
    ppermute x1 -> x0, waiting for transfers between devices: 9.54 us -> none  [body(): rowpart = lax.ppermute(piece, ('pair', 'row', 'col'), perm)]
    all_gather x0 -> x1, blocking collectives: none -> 6.16 us  [body(): every = lax.all_gather(own, 'col', axis=0)]
    unnamed x10 -> x0, local copies, waits for them, and re-layouts: 5.87 us -> none
    ppermute x1 -> x0, starting transfers between devices: 3.78 us -> none  [body(): rowpart = lax.ppermute(piece, ('pair', 'row', 'col'), perm)]
    pallas_call x3 -> x5, Pallas kernels: 21.7 us -> 25.3 us  [the longest x1 17.7 us: kernel1(): pl.pallas_call(transform_kernel, grid=(4,), in_specs=[smem, smem, smem, p...]
  transfers between devices with their start and end apart: 2 -> 0, of which waited for: 2 -> 0; matrix products, arithmetic and copies ran while one was open for 1% -> 0% of each run, Pallas kernels for 0% -> 0%
where the time goes in v2:
time: 94.3 us; the launch traced here: 93.1 us
  blocking collectives  66.4 us (70%)
  Pallas kernels  25.3 us (27%)
  other arithmetic  1.39 us (1%)
    all_to_all x1, blocking collectives, body(): lax.all_to_all(payload, 'pair', split_axis=0, concat_axis=0, tiled=True)  32.2 us
    pallas_call x1, Pallas kernels, kernel1(): pl.pallas_call(transform_kernel, grid=(4,), in_specs=[smem, smem, smem, p...  17.7 us
    all_to_all x1, blocking collectives, body(): lax.all_to_all(part, ('row', 'col'), split_axis=0, concat_axis=0, tiled=T...  14.8 us
    all_to_all x1, blocking collectives, body(): lax.all_to_all(tiles, 'row', split_axis=0, concat_axis=0, tiled=True)  13.2 us
    all_gather x1, blocking collectives, body(): every = lax.all_gather(own, 'col', axis=0)  6.16 us
    pallas_call x1, Pallas kernels, body(): pl.pallas_call(tile_kernel, in_specs=[VM], out_specs=VM, out_shape=jax.Sh...  2.21 us

profile of v2, /device:TPU:2, one launch (start us, length us, event | category | flops | bytes accessed | tf_op | source)
XLA Modules:
  0.0 93.1 jit_solution(4509310019348319836)
XLA Ops:
  0.0 1.4 %fusion.7 = (s32[4096]{0:T(1024)}, s32[4096]{0:T(1024)}) fusion(s32[4096]{0:T(1024)} %param.15), kind=kLoop, calls=%fused_computation.23 | loop fusion | flops 299008 | bytes 49152 | tf_op jit(solution)/shard_map/add | solution.py:165
  1.4 17.7 %partial_transform.1 = bf16[16,16,1024]{2,1,0:T(8,128)(2,1)} custom-call(s32[32]{0:T(128)} %val_s.3, s32[32]{0:T(128)} %con_s.3, s32[4096]{0:T(1024)} %get-tuple-element.6.row_s, bf16[32,49152]{1,0:T(8,128)(2,1)} %pv.1, bf16[64,49152]{1,0:T(8,128)(2,1)} %pc.1, s32[1,4096]{1,0:T(1,128)} %bitcast.5, bf16[2,208,512]{2,1,0:T(8,128)(2,1)} %constant.79.clone.ztab, ...), custom_call_target="tpu_custom_call" | custom-call | tf_op jit(solution)/shard_map/partial_transform/pallas_call | solution.py:169
  19.1 14.8 %all_to_all.15.parts = bf16[16,16,1024]{2,1,0:T(8,128)(2,1)} all-to-all(bf16[16,16,1024]{2,1,0:T(8,128)(2,1)} %partial_transform.1), channel_id=1, replica_groups=mesh['pair'=16,'row'=4,'col'=4] {'row','col'}, dimensions={0} | all-to-all | bytes 1048576 | tf_op jit(solution)/shard_map/all_to_all | solution.py:231
  33.9 1.7 %sum_parts.1.own = bf16[16,1024]{1,0:T(8,128)(2,1)} custom-call(bf16[16,16,1024]{2,1,0:T(8,128)(2,1)} %all_to_all.15.parts), custom_call_target="tpu_custom_call" | custom-call | tf_op jit(solution)/shard_map/sum_parts/pallas_call | solution.py:232
  35.6 6.2 %all-gather = bf16[64,1024]{1,0:T(8,128)(2,1)} all-gather(bf16[16,1024]{1,0:T(8,128)(2,1)} %sum_parts.1.own), channel_id=2, replica_groups=mesh['pair'=16,'row'=4,'col'=4] {'col'}, dimensions={0}, use_global_device_ids=true | all-gather | bytes 163840 | tf_op jit(solution)/shard_map/all_gather | solution.py:234
  41.8 1.8 %payload.1 = bf16[16,16,1280]{2,1,0:T(8,128)(2,1)} custom-call(s32[32]{0:T(128)} %val_s.3, s32[32]{0:T(128)} %con_s.3, f32[32]{0:T(128)} %ev_s.1, f32[64]{0:T(128)} %ec_s.1, bf16[16,1024]{1,0:T(8,128)(2,1)} %sum_parts.1.own, bf16[4,16,1024]{2,1,0:T(8,128)(2,1)} %bitcast.4), custom_call_target="tpu_custom_call" | custom-call | tf_op jit(solution)/shard_map/payload/pallas_call | solution.py:235
  43.6 32.2 %all_to_all.16 = bf16[16,16,1280]{2,1,0:T(8,128)(2,1)} all-to-all(bf16[16,16,1280]{2,1,0:T(8,128)(2,1)} %payload.1), channel_id=1, replica_groups=mesh['pair'=16,'row'=4,'col'=4] {'pair'}, dimensions={0} | all-to-all | bytes 1310720 | tf_op jit(solution)/shard_map/all_to_all | solution.py:237
  75.8 2.2 %tile.1 = bf16[4,64,1024]{2,1,0:T(8,128)(2,1)} custom-call(bf16[256,1280]{1,0:T(8,128)(2,1)} %bitcast.3), custom_call_target="tpu_custom_call" | custom-call | tf_op jit(solution)/shard_map/tile/pallas_call | solution.py:238
  78.0 13.2 %all_to_all.17.parts = bf16[4,64,1024]{2,1,0:T(8,128)(2,1)} all-to-all(bf16[4,64,1024]{2,1,0:T(8,128)(2,1)} %tile.1), channel_id=1, replica_groups=mesh['pair'=16,'row'=4,'col'=4] {'row'}, dimensions={0} | all-to-all | bytes 1048576 | tf_op jit(solution)/shard_map/all_to_all | solution.py:240
  91.3 1.8 %total.1 = f32[64,1024]{1,0:T(8,128)} custom-call(bf16[4,64,1024]{2,1,0:T(8,128)(2,1)} %all_to_all.17.parts), custom_call_target="tpu_custom_call" | custom-call | tf_op jit(solution)/shard_map/total/pallas_call | solution.py:241

commit v3 on v2

v3 whole, which is shorter than its diff:
```python
import math
import numpy as np
import jax, jax.numpy as jnp
from jax import lax
from jax.experimental import pallas as pl
from jax.experimental.pallas import tpu as pltpu
from jax.sharding import Mesh, PartitionSpec as P
import ml_dtypes
BF=ml_dtypes.bfloat16
GX=64;GY=64;GZ=192;NG=4096
KZ=104

def split_hi_lo(t):
    hi=t.astype(np.float32).astype(BF); lo=(t-hi.astype(np.float64)).astype(np.float32).astype(BF)
    return hi,lo

def z_tables():
    z=np.arange(GZ); k=np.arange(97)
    ang=2*np.pi/GZ*((k[:,None]*z[None,:])%GZ)
    t=np.zeros((2,KZ,GZ)); t[0,:97]=np.cos(ang); t[1,:97]=-np.sin(ang)
    t=t.reshape(2*KZ,GZ)
    out=np.zeros((2,2*KZ,512),BF)
    hi,lo=split_hi_lo(t)
    for par,off in ((0,0),(1,64)):
        out[par,:,off:off+GZ]=hi; out[par,:,256+off:256+off+GZ]=lo
    return out

def x_tables():
    factor=1.0/math.sqrt(GX*GY*GZ)
    out=np.zeros((16,16,256),BF)
    fx=np.arange(64)
    for d in range(16):
        xs=4*d+np.arange(4)
        ang=2*np.pi/GX*((fx[None,:]*xs[:,None])%GX)
        c=np.cos(ang)*factor; s=np.sin(ang)*factor
        for f,sig in ((0,1.0),(1,-1.0)):
            t=np.concatenate([c,sig*s,sig*c,-s],axis=0)
            hi,lo=split_hi_lo(t)
            out[d,:,f*64:(f+1)*64]=hi; out[d,:,128+f*64:128+(f+1)*64]=lo
    return out

def fft8(v):
    def add(a,b): return (a[0]+b[0],a[1]+b[1])
    def sub(a,b): return (a[0]-b[0],a[1]-b[1])
    def mi(a): return (a[1],-a[0])
    r=np.float32(math.sqrt(0.5))
    def fft4(x0,x1,x2,x3):
        a=add(x0,x2); b=sub(x0,x2); c=add(x1,x3); d=mi(sub(x1,x3))
        return add(a,c),add(b,d),sub(a,c),sub(b,d)
    e=fft4(v[0],v[2],v[4],v[6]); o=fft4(v[1],v[3],v[5],v[7])
    o1=((o[1][0]+o[1][1])*r,(o[1][1]-o[1][0])*r)
    o2=mi(o[2])
    o3=((o[3][1]-o[3][0])*r,-(o[3][0]+o[3][1])*r)
    os=(o[0],o1,o2,o3)
    return [add(e[k],os[k]) for k in range(4)]+[sub(e[k],os[k]) for k in range(4)]

def transform_kernel(val_s, con_s, ev_s, ec_s, pv, pc, gmap, ztab, xtabs, out, wout, rho, Z, Z2, GA, GB, xtab, rows_v, kcode, row_s, xsem, rsem):
    step=pl.program_id(0)
    place=lax.axis_index("row")*4+lax.axis_index("col")
    fetch=pltpu.make_async_copy(xtabs.at[place],xtab,xsem)
    move=pltpu.make_async_copy(rows_v,row_s,rsem)
    @pl.when(step==0)
    def _():
        fetch.start()
        g=gmap[...]
        q=((g.astype(jnp.float32)+0.5)*np.float32(1.0/GZ)).astype(jnp.int32)
        fz=g-q*GZ; fy=q&63; fx=q>>6
        flip=fz>96
        fz=jnp.where(flip,GZ-fz,fz)
        fy=jnp.where(flip,(64-fy)&63,fy)
        rows_v[...]=((fy&7)*8+(fy>>3))*(2*KZ)+2*fz
        kcode[...]=jnp.where(flip,64,0)+fx
        move.start()
        first=lax.axis_index("row")*8
        pid=lax.broadcasted_iota(jnp.int32,(16,128),0)%8
        ev=jnp.zeros((16,128),jnp.float32); ec=jnp.ones((16,128),jnp.float32)
        for p in range(8):
            ev=jnp.where(pid==p,ev_s[val_s[first+p]],ev)
            ec=jnp.where(pid==p,ec_s[con_s[first+p]],ec)
        wout[...]=-2.0/(math.sqrt(512)*(ec-ev))
    sub=lax.broadcasted_iota(jnp.int32,(64,96),0); lane=lax.broadcasted_iota(jnp.int32,(64,96),1)
    want=jnp.zeros((64,96),jnp.int32)
    for p in range(32):
        want=jnp.where(sub==p, val_s[p], want)
        want=jnp.where(sub==32+p, con_s[p]+32, want)
    sel=(want==lane).astype(jnp.bfloat16)
    CH=512
    for u in range(12288//CH):
        o=u*CH
        src=jnp.concatenate([pv[:,o:o+CH],pc[:,o:o+CH]],axis=0)
        res=jnp.dot(sel,src,preferred_element_type=jnp.float32)
        rho[step,:,o:o+CH]=(res[:32]*res[32:]).astype(jnp.bfloat16)

    @pl.when(step==3)
    def _():
        fetch.wait()
        move.wait()
        for b in range(8):
            wt=ztab[b%2]
            for ah in range(4):
                parts=[]
                for a in (2*ah,2*ah+1):
                    yp=4*a+b//2; o=384*yp+128*(b%2)
                    for x in range(4):
                        parts.append(rho[x,:,o:o+256])
                B=jnp.concatenate(parts,axis=0)
                B=jnp.concatenate([B,B],axis=1)
                res=lax.dot_general(wt,B,(((1,),(1,)),((),())),preferred_element_type=jnp.float32)
                Z[pl.ds((8*(2*ah)+b)*2*KZ,2*KZ),:]=res[:,:128]
                Z[pl.ds((8*(2*ah+1)+b)*2*KZ,2*KZ),:]=res[:,128:]
        tw=[[np.exp(-2j*np.pi*b*k/64) for k in range(8)] for b in range(8)]
        def pass1(j,_):
            r0=pl.multiple_of(j*8,8)
            for b in range(8):
                v=[(Z[pl.ds((8*a+b)*2*KZ+r0,8),:],Z[pl.ds((8*a+b)*2*KZ+KZ+r0,8),:]) for a in range(8)]
                w=fft8(v)
                for k in range(8):
                    re,im=w[k]
                    if b and k:
                        c=np.float32(tw[b][k].real); s=np.float32(tw[b][k].imag)
                        re,im=re*c-im*s, re*s+im*c
                    Z[pl.ds((8*k+b)*2*KZ+r0,8),:]=re; Z[pl.ds((8*k+b)*2*KZ+KZ+r0,8),:]=im
            return 0
        lax.fori_loop(0,KZ//8,pass1,0)
        def pass2(j,_):
            r0=pl.multiple_of(j*8,8)
            for k1 in range(8):
                v=[(Z[pl.ds((8*k1+b)*2*KZ+r0,8),:],Z[pl.ds((8*k1+b)*2*KZ+KZ+r0,8),:]) for b in range(8)]
                w=fft8(v)
                for k in range(8):
                    re,im=w[k]
                    base=(8*k1+k)*2*KZ+2*r0
                    Z2[pl.ds(base,8,stride=2),:]=re; Z2[pl.ds(base+1,8,stride=2),:]=im
            return 0
        lax.fori_loop(0,KZ//8,pass2,0)
        ksub=lax.broadcasted_iota(jnp.int32,(128,128),0)
        def gather(t,G):
            for j in range(256):
                rr=pl.multiple_of(row_s[2*t+j//128,j%128],2)
                G[pl.ds(2*j,2),:]=Z2[pl.ds(rr,2),:]
        def phase(t,G):
            c=t//4
            for h in range(2):
                oh=(ksub==kcode[pl.ds(2*t+h,1),:]).astype(jnp.bfloat16)
                oh=jnp.concatenate([oh,oh],axis=0)
                co=jnp.dot(xtab[...],oh,preferred_element_type=jnp.float32)
                R=G[pl.ds(256*h,128,stride=2),:].T; I=G[pl.ds(256*h+1,128,stride=2),:].T
                re=0.0; im=0.0
                for x in range(4):
                    rx=R[32*x:32*x+32]; ix=I[32*x:32*x+32]
                    re=re+co[x:x+1]*rx+co[4+x:5+x]*ix
                    im=im+co[8+x:9+x]*ix+co[12+x:13+x]*rx
                at=pl.multiple_of((t%4)*256+h*128,128)
                for r in range(4):
                    both=jnp.concatenate([re[8*r:8*r+8],im[8*r:8*r+8]],axis=0)
                    out[r*4+c,:,pl.ds(at,128)]=both.astype(jnp.bfloat16)
        gather(0,GA)
        def pairs(u,_):
            t=2*u
            gather(t+1,GB); phase(t,GA)
            gather(jnp.minimum(t+2,15),GA); phase(t+1,GB)
            return 0
        lax.fori_loop(0,8,pairs,0)

def partial_transform(val_idx,con_idx,e_val,e_con,pv,pc,gmap):
    smem=pl.BlockSpec(memory_space=pltpu.SMEM)
    return pl.pallas_call(
        transform_kernel,
        grid=(4,),
        in_specs=[smem,smem,smem,smem,
                  pl.BlockSpec((32,12288),lambda i:(0,i)),
                  pl.BlockSpec((64,12288),lambda i:(0,i)),
                  pl.BlockSpec((32,128),lambda i:(0,0)),
                  pl.BlockSpec((2,2*KZ,512),lambda i:(0,0,0)),
                  pl.BlockSpec(memory_space=pl.ANY)],
        out_specs=[pl.BlockSpec((16,16,1024),lambda i:(0,0,0)),pl.BlockSpec((16,128),lambda i:(0,0))],
        scratch_shapes=[pltpu.VMEM((4,32,12288),jnp.bfloat16),
                        pltpu.VMEM((64*2*KZ,128),jnp.float32),
                        pltpu.VMEM((64*2*KZ,128),jnp.float32),
                        pltpu.VMEM((512,128),jnp.float32),
                        pltpu.VMEM((512,128),jnp.float32),
                        pltpu.VMEM((16,256),jnp.bfloat16),
                        pltpu.VMEM((32,128),jnp.int32),
                        pltpu.VMEM((32,128),jnp.int32),
                        pltpu.SMEM((32,128),jnp.int32),
                        pltpu.SemaphoreType.DMA,
                        pltpu.SemaphoreType.DMA],
        out_shape=[jax.ShapeDtypeStruct((16,16,1024),jnp.bfloat16),jax.ShapeDtypeStruct((16,128),jnp.float32)],
        compiler_params=pltpu.CompilerParams(vmem_limit_bytes=60*2**20, dimension_semantics=("arbitrary",)),
        name="partial_transform",
    )(val_idx,con_idx,e_val,e_con,pv,pc,gmap.reshape(32,128),jnp.asarray(z_tables()),jnp.asarray(x_tables()))

def body(psi_val, psi_con, e_val, e_con, val_idx, con_idx, gmap):
    part,w=partial_transform(val_idx,con_idx,e_val,e_con,psi_val,psi_con,gmap)
    recv=lax.all_to_all(part,("row","col"),split_axis=0,concat_axis=0,tiled=True)
    own=recv.astype(jnp.float32).sum(0).astype(jnp.bfloat16)
    every=lax.all_gather(own,"col",axis=0)
    weighted=(every.astype(jnp.float32)*w[None,:,:1]).astype(jnp.bfloat16)
    rowside=weighted.reshape(4,16,2,512).transpose(0,2,1,3).reshape(8,1,16,512)
    colside=own.reshape(16,2,512).transpose(1,0,2).reshape(1,2,16,512)
    payload=jnp.concatenate([jnp.broadcast_to(colside,(8,2,16,512)),jnp.broadcast_to(rowside,(8,2,16,512))],axis=3).reshape(16,16,1024)
    groups=lax.all_to_all(payload,("ph","pl"),split_axis=0,concat_axis=0,tiled=True).reshape(256,1024)
    tiles=lax.dot_general(groups[:,512:],groups[:,:512],(((0,),(0,)),((),())),preferred_element_type=jnp.float32).astype(jnp.bfloat16)
    tiles=lax.all_to_all(tiles.reshape(8,64,512),("pl","row"),split_axis=0,concat_axis=0,tiled=True)
    sums=tiles.reshape(2,4,64,512).astype(jnp.float32).sum(1)
    return jnp.concatenate([sums[0],sums[1]],axis=1)

def solution(mesh):
    fine=Mesh(mesh.devices.reshape(8,2,4,4),("ph","pl","row","col"))
    pair=("ph","pl")
    return jax.shard_map(
        body,
        mesh=fine,
        in_specs=(
            P(None, ("row", "col")),
            P(None, ("row", "col")),
            P(),
            P(),
            P(pair),
            P(pair),
            P(),
        ),
        out_specs=P(("ph","pl","row"), "col"),
        check_vma=False,
    )
```

time: 94.3 us -> 78.1 us (0.83)
  blocking collectives: 66.4 us -> 45.6 us
  Pallas kernels: 25.3 us -> 16.1 us
  waiting for transfers between devices: 0 us -> 7.68 us
  starting transfers between devices: 0 us -> 5.87 us
    all_to_all x3 -> x2, blocking collectives: 60.2 us -> 40.2 us  [the longest x1 28.1 us: body(): lax.all_to_all(payload, ('ph', 'pl'), split_axis=0, concat_axis=0, tiled=...]
    pallas_call x5 -> x1, Pallas kernels: 25.3 us -> 16.1 us  [partial_transform(): pl.pallas_call(transform_kernel, grid=(4,), in_specs=[smem, smem, smem, s...]
    all_to_all x0 -> x1, waiting for transfers between devices: none -> 7.68 us  [body(): lax.all_to_all(part, ('row', 'col'), split_axis=0, concat_axis=0, tiled=T...]
    all_to_all x0 -> x1, starting transfers between devices: none -> 5.87 us  [body(): lax.all_to_all(part, ('row', 'col'), split_axis=0, concat_axis=0, tiled=T...]
    add x1 -> x0, other arithmetic: 1.39 us -> none  [prep(): return (rows, flag * 64 + fx)]
  transfers between devices with their start and end apart: 0 -> 1, of which waited for: 0 -> 1; matrix products, arithmetic and copies ran while one was open for 0% -> 1% of each run, Pallas kernels for 0% -> 0%
where the time goes in v3:
time: 78.1 us; the launch traced here: 77.6 us
  blocking collectives  45.6 us (58%)
  Pallas kernels  16.1 us (21%)
  waiting for transfers between devices  7.68 us (10%)
  starting transfers between devices  5.87 us (8%)
  other arithmetic  1.02 us (1%)
  local copies, waits for them, and re-layouts  0.91 us (1%)
    all_to_all x1, blocking collectives, body(): lax.all_to_all(payload, ('ph', 'pl'), split_axis=0, concat_axis=0, tiled=...  28.1 us
    pallas_call x1, Pallas kernels, partial_transform(): pl.pallas_call(transform_kernel, grid=(4,), in_specs=[smem, smem, smem, s...  16.1 us
    all_to_all x1, blocking collectives, body(): lax.all_to_all(tiles.reshape(8, 64, 512), ('pl', 'row'), split_axis=0, co...  12.1 us
    all_to_all x1, waiting for transfers between devices, body(): lax.all_to_all(part, ('row', 'col'), split_axis=0, concat_axis=0, tiled=T...  7.68 us
    all_to_all x1, starting transfers between devices, body(): lax.all_to_all(part, ('row', 'col'), split_axis=0, concat_axis=0, tiled=T...  5.87 us
    all_gather x1, blocking collectives, body(): every = lax.all_gather(own, 'col', axis=0)  5.43 us
  transfers between devices with their start and end apart: 1, of which 1 were waited for; matrix products, arithmetic and copies ran while one was open for 1% of the time, Pallas kernels for 0%

profile of v3, /device:TPU:2, one launch (start us, length us, event | category | flops | bytes accessed | tf_op | source)
XLA Modules:
  0.0 77.6 jit_solution(6612230042854073828)
XLA Ops:
  0.0 16.1 %partial_transform.1 = (bf16[16,16,1024]{2,1,0:T(8,128)(2,1)}, f32[16,128]{1,0:T(8,128)}) custom-call(s32[32]{0:T(128)} %val_s.1, s32[32]{0:T(128)} %con_s.1, f32[32]{0:T(128)} %ev_s.1, f32[64]{0:T(128)} %ec_s.1, bf16[32,49152]{1,0:T(8,128)(2,1)} %pv.1, bf16[64,49152]{1,0:T(8,128)(2,1)} %pc.1, s32[32,128]{1,0:T(8,128)} %bitcast.21, ...), custom_call_target="tpu_custom_call" | custom-call | tf_op jit(solution)/shard_map/partial_transform/pallas_call | solution.py:167
  16.2 5.9 %all-to-all-start = ((bf16[16,16,1024]{2,1,0:T(8,128)(2,1)}), bf16[16,16,1024]{2,1,0:T(8,128)(2,1)S(1)}, u32[]{:S(2)}, u32[]{:S(2)}) async-start(bf16[16,16,1024]{2,1,0:T(8,128)(2,1)} %get-tuple-element.7), calls=%async_computation | async-start | bytes 1048576 | tf_op jit(solution)/shard_map/all_to_all | solution.py:195
  22.0 0.8 %slice_reduce_fusion = f32[16]{0:T(128)S(1)} fusion(f32[16,128]{1,0:T(8,128)} %get-tuple-element.8), kind=kLoop, calls=%fused_computation.11 | loop fusion | bytes 128 | tf_op jit(solution)/shard_map/slice | solution.py:198
  22.8 7.7 %all-to-all-done = bf16[16,16,1024]{2,1,0:T(8,128)(2,1)S(1)} async-done(((bf16[16,16,1024]{2,1,0:T(8,128)(2,1)}), bf16[16,16,1024]{2,1,0:T(8,128)(2,1)S(1)}, u32[]{:S(2)}, u32[]{:S(2)}) %all-to-all-start) | async-done | bytes 524320 | tf_op jit(solution)/shard_map/all_to_all | solution.py:195
  30.5 0.1 reduce_sum.21
  30.6 5.4 %all-gather = bf16[64,1024]{1,0:T(8,128)(2,1)S(1)} all-gather(bf16[16,1024]{1,0:T(8,128)(2,1)S(1)} %reduce_sum.21), channel_id=2, replica_groups=mesh['ph'=8,'pl'=2,'row'=4,'col'=4] {'col'}, dimensions={0}, use_global_device_ids=true | all-gather | bytes 163840 | tf_op jit(solution)/shard_map/all_gather | solution.py:197
  36.1 0.1 fusion.2
  36.2 0.1 pad_maximum_fusion
  36.3 28.1 %all_to_all.15 = bf16[16,16,1024]{2,1,0:T(8,128)(2,1)S(1)} all-to-all(bf16[16,16,1024]{2,1,0:T(8,128)(2,1)S(1)} %bitcast.15), channel_id=1, replica_groups=mesh['ph'=8,'pl'=2,'row'=4,'col'=4] {'ph','pl'}, dimensions={0} | all-to-all | bytes 1048576 | tf_op jit(solution)/shard_map/all_to_all | solution.py:202
  64.4 0.3 convolution_convert_fusion
  64.8 12.1 %all_to_all.16 = bf16[8,64,512]{2,1,0:T(8,128)(2,1)S(1)} all-to-all(bf16[8,64,512]{2,1,0:T(8,128)(2,1)S(1)} %bitcast.19), channel_id=1, replica_groups=mesh['ph'=8,'pl'=2,'row'=4,'col'=4] {'pl','row'}, dimensions={0} | all-to-all | bytes 1048576 | tf_op jit(solution)/shard_map/all_to_all | solution.py:204
  76.8 0.1 convert_reduce_fusion
  76.9 0.7 pad_maximum_fusion.1
  (7 shorter events, 0.1 us)
Async XLA Ops:
  16.2 14.4 %all-to-all-start = ((bf16[16,16,1024]{2,1,0:T(8,128)(2,1)}), bf16[16,16,1024]{2,1,0:T(8,128)(2,1)S(1)}, u32[]{:S(2)}, u32[]{:S(2)}) async-start(bf16[16,16,1024]{2,1,0:T(8,128)(2,1)} %get-tuple-element.7), calls=%async_computation | async-start | bytes 1048576 | tf_op jit(solution)/shard_map/all_to_all | solution.py:195

commit v4 on v3

v4 whole, which is shorter than its diff:
```python
import math
import numpy as np
import jax, jax.numpy as jnp
from jax import lax
from jax.experimental import pallas as pl
from jax.experimental.pallas import tpu as pltpu
from jax.sharding import Mesh, PartitionSpec as P
import ml_dtypes
BF=ml_dtypes.bfloat16
GX=64;GY=64;GZ=192;NG=4096
KZ=104

def split_hi_lo(t):
    hi=t.astype(np.float32).astype(BF); lo=(t-hi.astype(np.float64)).astype(np.float32).astype(BF)
    return hi,lo

def z_tables():
    z=np.arange(GZ); k=np.arange(97)
    ang=2*np.pi/GZ*((k[:,None]*z[None,:])%GZ)
    t=np.zeros((2,KZ,GZ)); t[0,:97]=np.cos(ang); t[1,:97]=-np.sin(ang)
    t=t.reshape(2*KZ,GZ)
    out=np.zeros((2,2*KZ,512),BF)
    hi,lo=split_hi_lo(t)
    for par,off in ((0,0),(1,64)):
        out[par,:,off:off+GZ]=hi; out[par,:,256+off:256+off+GZ]=lo
    return out

def x_tables():
    factor=1.0/math.sqrt(GX*GY*GZ)
    out=np.zeros((16,16,256),BF)
    fx=np.arange(64)
    for d in range(16):
        xs=4*d+np.arange(4)
        ang=2*np.pi/GX*((fx[None,:]*xs[:,None])%GX)
        c=np.cos(ang)*factor; s=np.sin(ang)*factor
        for f,sig in ((0,1.0),(1,-1.0)):
            t=np.concatenate([c,sig*s,sig*c,-s],axis=0)
            hi,lo=split_hi_lo(t)
            out[d,:,f*64:(f+1)*64]=hi; out[d,:,128+f*64:128+(f+1)*64]=lo
    return out

def fft8(v):
    def add(a,b): return (a[0]+b[0],a[1]+b[1])
    def sub(a,b): return (a[0]-b[0],a[1]-b[1])
    def mi(a): return (a[1],-a[0])
    r=np.float32(math.sqrt(0.5))
    def fft4(x0,x1,x2,x3):
        a=add(x0,x2); b=sub(x0,x2); c=add(x1,x3); d=mi(sub(x1,x3))
        return add(a,c),add(b,d),sub(a,c),sub(b,d)
    e=fft4(v[0],v[2],v[4],v[6]); o=fft4(v[1],v[3],v[5],v[7])
    o1=((o[1][0]+o[1][1])*r,(o[1][1]-o[1][0])*r)
    o2=mi(o[2])
    o3=((o[3][1]-o[3][0])*r,-(o[3][0]+o[3][1])*r)
    os=(o[0],o1,o2,o3)
    return [add(e[k],os[k]) for k in range(4)]+[sub(e[k],os[k]) for k in range(4)]

def transform_kernel(val_s, con_s, ev_s, ec_s, pv, pc, gmap, ztab, xtabs, out, wout, va, vb, rho, Z, Z2, GA, GB, xtab, rows_v, kcode, row_s, asem, bsem, xsem, rsem):
    place=lax.axis_index("row")*4+lax.axis_index("col")
    planes=[(pltpu.make_async_copy(pv.at[:,pl.ds(12288*x,12288)],va.at[x],asem.at[x]),
             pltpu.make_async_copy(pc.at[:,pl.ds(12288*x,12288)],vb.at[x],bsem.at[x])) for x in range(4)]
    for one in planes:
        one[0].start()
        one[1].start()
    fetch=pltpu.make_async_copy(xtabs.at[place],xtab,xsem)
    fetch.start()
    g=gmap[...]
    q=((g.astype(jnp.float32)+0.5)*np.float32(1.0/GZ)).astype(jnp.int32)
    fz=g-q*GZ; fy=q&63; fx=q>>6
    flip=fz>96
    fz=jnp.where(flip,GZ-fz,fz)
    fy=jnp.where(flip,(64-fy)&63,fy)
    rows_v[...]=((fy&7)*8+(fy>>3))*(2*KZ)+2*fz
    kcode[...]=jnp.where(flip,64,0)+fx
    move=pltpu.make_async_copy(rows_v,row_s,rsem)
    move.start()
    first=lax.axis_index("row")*8
    pid=lax.broadcasted_iota(jnp.int32,(16,128),0)%8
    ev=jnp.zeros((16,128),jnp.float32); ec=jnp.ones((16,128),jnp.float32)
    for p in range(8):
        ev=jnp.where(pid==p,ev_s[val_s[first+p]],ev)
        ec=jnp.where(pid==p,ec_s[con_s[first+p]],ec)
    wout[...]=-2.0/(math.sqrt(512)*(ec-ev))
    sub=lax.broadcasted_iota(jnp.int32,(8,96),0); lane=lax.broadcasted_iota(jnp.int32,(8,96),1)
    picks=[]
    for q in range(8):
        want=jnp.zeros((8,96),jnp.int32)
        for k in range(8):
            p=8*q+k
            want=jnp.where(sub==k, val_s[p] if p<32 else con_s[p-32]+32, want)
        picks.append((want==lane).astype(jnp.float32))
    sel=jnp.concatenate(picks,axis=0).astype(jnp.bfloat16)
    CH=512
    for x in range(4):
        planes[x][0].wait()
        planes[x][1].wait()
        for u in range(12288//CH):
            o=u*CH
            src=jnp.concatenate([va[x,:,o:o+CH],vb[x,:,o:o+CH]],axis=0)
            res=jnp.dot(sel,src,preferred_element_type=jnp.float32)
            rho[x,:,o:o+CH]=(res[:32]*res[32:]).astype(jnp.bfloat16)
    fetch.wait()
    move.wait()
    for b in range(8):
        wt=ztab[b%2]
        for ah in range(4):
            parts=[]
            for a in (2*ah,2*ah+1):
                yp=4*a+b//2; o=384*yp+128*(b%2)
                for x in range(4):
                    parts.append(rho[x,:,o:o+256])
            B=jnp.concatenate(parts,axis=0)
            B=jnp.concatenate([B,B],axis=1)
            res=lax.dot_general(wt,B,(((1,),(1,)),((),())),preferred_element_type=jnp.float32)
            Z[pl.ds((8*(2*ah)+b)*2*KZ,2*KZ),:]=res[:,:128]
            Z[pl.ds((8*(2*ah+1)+b)*2*KZ,2*KZ),:]=res[:,128:]
    tw=[[np.exp(-2j*np.pi*b*k/64) for k in range(8)] for b in range(8)]
    def pass1(j,_):
        r0=pl.multiple_of(j*8,8)
        for b in range(8):
            v=[(Z[pl.ds((8*a+b)*2*KZ+r0,8),:],Z[pl.ds((8*a+b)*2*KZ+KZ+r0,8),:]) for a in range(8)]
            w=fft8(v)
            for k in range(8):
                re,im=w[k]
                if b and k:
                    c=np.float32(tw[b][k].real); s=np.float32(tw[b][k].imag)
                    re,im=re*c-im*s, re*s+im*c
                Z[pl.ds((8*k+b)*2*KZ+r0,8),:]=re; Z[pl.ds((8*k+b)*2*KZ+KZ+r0,8),:]=im
        return 0
    lax.fori_loop(0,KZ//8,pass1,0)
    def pass2(j,_):
        r0=pl.multiple_of(j*8,8)
        for k1 in range(8):
            v=[(Z[pl.ds((8*k1+b)*2*KZ+r0,8),:],Z[pl.ds((8*k1+b)*2*KZ+KZ+r0,8),:]) for b in range(8)]
            w=fft8(v)
            for k in range(8):
                re,im=w[k]
                base=(8*k1+k)*2*KZ+2*r0
                Z2[pl.ds(base,8,stride=2),:]=re; Z2[pl.ds(base+1,8,stride=2),:]=im
        return 0
    lax.fori_loop(0,KZ//8,pass2,0)
    ksub=lax.broadcasted_iota(jnp.int32,(128,128),0)
    def gather(t,G):
        for j in range(256):
            rr=pl.multiple_of(row_s[2*t+j//128,j%128],2)
            G[pl.ds(2*j,2),:]=Z2[pl.ds(rr,2),:]
    def phase(t,G):
        c=t//4
        for h in range(2):
            oh=(ksub==kcode[pl.ds(2*t+h,1),:]).astype(jnp.bfloat16)
            oh=jnp.concatenate([oh,oh],axis=0)
            co=jnp.dot(xtab[...],oh,preferred_element_type=jnp.float32)
            R=G[pl.ds(256*h,128,stride=2),:].T; I=G[pl.ds(256*h+1,128,stride=2),:].T
            re=0.0; im=0.0
            for x in range(4):
                rx=R[32*x:32*x+32]; ix=I[32*x:32*x+32]
                re=re+co[x:x+1]*rx+co[4+x:5+x]*ix
                im=im+co[8+x:9+x]*ix+co[12+x:13+x]*rx
            at=pl.multiple_of((t%4)*256+h*128,128)
            for r in range(4):
                both=jnp.concatenate([re[8*r:8*r+8],im[8*r:8*r+8]],axis=0)
                out[r*4+c,:,pl.ds(at,128)]=both.astype(jnp.bfloat16)
    gather(0,GA)
    for t in range(16):
        if t<15:
            gather(t+1,(GA,GB)[(t+1)%2])
        phase(t,(GA,GB)[t%2])

def partial_transform(val_idx,con_idx,e_val,e_con,pv,pc,gmap):
    smem=pl.BlockSpec(memory_space=pltpu.SMEM)
    return pl.pallas_call(
        transform_kernel,
        grid=(1,),
        in_specs=[smem,smem,smem,smem,
                  pl.BlockSpec(memory_space=pl.ANY),
                  pl.BlockSpec(memory_space=pl.ANY),
                  pl.BlockSpec((32,128),lambda i:(0,0)),
                  pl.BlockSpec((2,2*KZ,512),lambda i:(0,0,0)),
                  pl.BlockSpec(memory_space=pl.ANY)],
        out_specs=[pl.BlockSpec((16,16,1024),lambda i:(0,0,0)),pl.BlockSpec((16,128),lambda i:(0,0))],
        scratch_shapes=[pltpu.VMEM((4,32,12288),jnp.bfloat16),
                        pltpu.VMEM((4,64,12288),jnp.bfloat16),
                        pltpu.VMEM((4,32,12288),jnp.bfloat16),
                        pltpu.VMEM((64*2*KZ,128),jnp.float32),
                        pltpu.VMEM((64*2*KZ,128),jnp.float32),
                        pltpu.VMEM((512,128),jnp.float32),
                        pltpu.VMEM((512,128),jnp.float32),
                        pltpu.VMEM((16,256),jnp.bfloat16),
                        pltpu.VMEM((32,128),jnp.int32),
                        pltpu.VMEM((32,128),jnp.int32),
                        pltpu.SMEM((32,128),jnp.int32),
                        pltpu.SemaphoreType.DMA((4,)),
                        pltpu.SemaphoreType.DMA((4,)),
                        pltpu.SemaphoreType.DMA,
                        pltpu.SemaphoreType.DMA],
        out_shape=[jax.ShapeDtypeStruct((16,16,1024),jnp.bfloat16),jax.ShapeDtypeStruct((16,128),jnp.float32)],
        compiler_params=pltpu.CompilerParams(vmem_limit_bytes=60*2**20, dimension_semantics=("arbitrary",)),
        name="partial_transform",
    )(val_idx,con_idx,e_val,e_con,pv,pc,gmap.reshape(32,128),jnp.asarray(z_tables()),jnp.asarray(x_tables()))

def body(psi_val, psi_con, e_val, e_con, val_idx, con_idx, gmap):
    part,w=partial_transform(val_idx,con_idx,e_val,e_con,psi_val,psi_con,gmap)
    recv=lax.all_to_all(part,("row","col"),split_axis=0,concat_axis=0,tiled=True)
    own=recv.astype(jnp.float32).sum(0).astype(jnp.bfloat16)
    every=lax.all_gather(own,"col",axis=0)
    weighted=(every.astype(jnp.float32)*w[None,:,:1]).astype(jnp.bfloat16)
    rowside=weighted.reshape(4,16,2,512).transpose(0,2,1,3).reshape(8,1,16,512)
    colside=own.reshape(16,2,512).transpose(1,0,2).reshape(1,2,16,512)
    payload=jnp.concatenate([jnp.broadcast_to(colside,(8,2,16,512)),jnp.broadcast_to(rowside,(8,2,16,512))],axis=3).reshape(16,16,1024)
    groups=lax.all_to_all(payload,("ph","pl"),split_axis=0,concat_axis=0,tiled=True).reshape(256,1024)
    tiles=lax.dot_general(groups[:,512:],groups[:,:512],(((0,),(0,)),((),())),preferred_element_type=jnp.float32).astype(jnp.bfloat16)
    tiles=lax.all_to_all(tiles.reshape(8,64,512),("pl","row"),split_axis=0,concat_axis=0,tiled=True)
    sums=tiles.reshape(2,4,64,512).astype(jnp.float32).sum(1)
    return jnp.concatenate([sums[0],sums[1]],axis=1)

def solution(mesh):
    fine=Mesh(mesh.devices.reshape(8,2,4,4),("ph","pl","row","col"))
    pair=("ph","pl")
    return jax.shard_map(
        body,
        mesh=fine,
        in_specs=(
            P(None, ("row", "col")),
            P(None, ("row", "col")),
            P(),
            P(),
            P(pair),
            P(pair),
            P(),
        ),
        out_specs=P(("ph","pl","row"), "col"),
        check_vma=False,
    )
```

time: 78.1 us -> 76.7 us (0.982)
  Pallas kernels: 16.1 us -> 14.8 us
    pallas_call x1, Pallas kernels: 16.1 us -> 14.8 us  [partial_transform(): pl.pallas_call(transform_kernel, grid=(1,), in_specs=[smem, smem, smem, s...]
where the time goes in v4:
time: 76.7 us; the launch traced here: 76.3 us
  blocking collectives  45.6 us (59%)
  Pallas kernels  14.8 us (19%)
  waiting for transfers between devices  7.68 us (10%)
  starting transfers between devices  5.91 us (8%)
  other arithmetic  1.02 us (1%)
  local copies, waits for them, and re-layouts  0.91 us (1%)
    all_to_all x1, blocking collectives, body(): lax.all_to_all(payload, ('ph', 'pl'), split_axis=0, concat_axis=0, tiled=...  28.1 us
    pallas_call x1, Pallas kernels, partial_transform(): pl.pallas_call(transform_kernel, grid=(1,), in_specs=[smem, smem, smem, s...  14.8 us
    all_to_all x1, blocking collectives, body(): lax.all_to_all(tiles.reshape(8, 64, 512), ('pl', 'row'), split_axis=0, co...  12.1 us
    all_to_all x1, waiting for transfers between devices, body(): lax.all_to_all(part, ('row', 'col'), split_axis=0, concat_axis=0, tiled=T...  7.68 us
    all_to_all x1, starting transfers between devices, body(): lax.all_to_all(part, ('row', 'col'), split_axis=0, concat_axis=0, tiled=T...  5.91 us
    all_gather x1, blocking collectives, body(): every = lax.all_gather(own, 'col', axis=0)  5.43 us
  transfers between devices with their start and end apart: 1, of which 1 were waited for; matrix products, arithmetic and copies ran while one was open for 1% of the time, Pallas kernels for 0%

profile of v4, /device:TPU:2, one launch (start us, length us, event | category | flops | bytes accessed | tf_op | source)
XLA Modules:
  0.0 76.3 jit_solution(13247223029522885825)
XLA Ops:
  0.0 14.8 %partial_transform.1 = (bf16[16,16,1024]{2,1,0:T(8,128)(2,1)}, f32[16,128]{1,0:T(8,128)}) custom-call(s32[32]{0:T(128)} %val_s.1, s32[32]{0:T(128)} %con_s.1, f32[32]{0:T(128)} %ev_s.1, f32[64]{0:T(128)} %ec_s.1, bf16[32,49152]{1,0:T(8,128)(2,1)} %pv.1, bf16[64,49152]{1,0:T(8,128)(2,1)} %pc.1, s32[32,128]{1,0:T(8,128)} %bitcast.21, ...), custom_call_target="tpu_custom_call" | custom-call | tf_op jit(solution)/shard_map/partial_transform/pallas_call | solution.py:170
  14.8 5.9 %all-to-all-start = ((bf16[16,16,1024]{2,1,0:T(8,128)(2,1)}), bf16[16,16,1024]{2,1,0:T(8,128)(2,1)S(1)}, u32[]{:S(2)}, u32[]{:S(2)}) async-start(bf16[16,16,1024]{2,1,0:T(8,128)(2,1)} %get-tuple-element.7), calls=%async_computation | async-start | bytes 1048576 | tf_op jit(solution)/shard_map/all_to_all | solution.py:202
  20.7 0.8 %slice_reduce_fusion = f32[16]{0:T(128)S(1)} fusion(f32[16,128]{1,0:T(8,128)} %get-tuple-element.8), kind=kLoop, calls=%fused_computation.11 | loop fusion | bytes 128 | tf_op jit(solution)/shard_map/slice | solution.py:205
  21.5 7.7 %all-to-all-done = bf16[16,16,1024]{2,1,0:T(8,128)(2,1)S(1)} async-done(((bf16[16,16,1024]{2,1,0:T(8,128)(2,1)}), bf16[16,16,1024]{2,1,0:T(8,128)(2,1)S(1)}, u32[]{:S(2)}, u32[]{:S(2)}) %all-to-all-start) | async-done | bytes 524320 | tf_op jit(solution)/shard_map/all_to_all | solution.py:202
  29.2 0.1 reduce_sum.21
  29.3 5.4 %all-gather = bf16[64,1024]{1,0:T(8,128)(2,1)S(1)} all-gather(bf16[16,1024]{1,0:T(8,128)(2,1)S(1)} %reduce_sum.21), channel_id=2, replica_groups=mesh['ph'=8,'pl'=2,'row'=4,'col'=4] {'col'}, dimensions={0}, use_global_device_ids=true | all-gather | bytes 163840 | tf_op jit(solution)/shard_map/all_gather | solution.py:204
  34.7 0.1 fusion.2
  34.9 0.1 pad_maximum_fusion
  35.0 28.1 %all_to_all.15 = bf16[16,16,1024]{2,1,0:T(8,128)(2,1)S(1)} all-to-all(bf16[16,16,1024]{2,1,0:T(8,128)(2,1)S(1)} %bitcast.15), channel_id=1, replica_groups=mesh['ph'=8,'pl'=2,'row'=4,'col'=4] {'ph','pl'}, dimensions={0} | all-to-all | bytes 1048576 | tf_op jit(solution)/shard_map/all_to_all | solution.py:209
  63.1 0.3 convolution_convert_fusion
  63.4 12.1 %all_to_all.16 = bf16[8,64,512]{2,1,0:T(8,128)(2,1)S(1)} all-to-all(bf16[8,64,512]{2,1,0:T(8,128)(2,1)S(1)} %bitcast.19), channel_id=1, replica_groups=mesh['ph'=8,'pl'=2,'row'=4,'col'=4] {'pl','row'}, dimensions={0} | all-to-all | bytes 1048576 | tf_op jit(solution)/shard_map/all_to_all | solution.py:211
  75.5 0.1 convert_reduce_fusion
  75.6 0.7 pad_maximum_fusion.1
  (7 shorter events, 0.1 us)
Async XLA Ops:
  14.8 14.4 %all-to-all-start = ((bf16[16,16,1024]{2,1,0:T(8,128)(2,1)}), bf16[16,16,1024]{2,1,0:T(8,128)(2,1)S(1)}, u32[]{:S(2)}, u32[]{:S(2)}) async-start(bf16[16,16,1024]{2,1,0:T(8,128)(2,1)} %get-tuple-element.7), calls=%async_computation | async-start | bytes 1048576 | tf_op jit(solution)/shard_map/all_to_all | solution.py:202

commit v5 on v4

--- a/solution.py
+++ b/solution.py
@@ -19,10 +19,10 @@
     ang=2*np.pi/GZ*((k[:,None]*z[None,:])%GZ)
     t=np.zeros((2,KZ,GZ)); t[0,:97]=np.cos(ang); t[1,:97]=-np.sin(ang)
     t=t.reshape(2*KZ,GZ)
-    out=np.zeros((2,2*KZ,512),BF)
+    out=np.zeros((2,4*KZ,256),BF)
     hi,lo=split_hi_lo(t)
     for par,off in ((0,0),(1,64)):
-        out[par,:,off:off+GZ]=hi; out[par,:,256+off:256+off+GZ]=lo
+        out[par,:2*KZ,off:off+GZ]=hi; out[par,2*KZ:,off:off+GZ]=lo
     return out
 
 def x_tables():
@@ -102,17 +102,17 @@
     move.wait()
     for b in range(8):
         wt=ztab[b%2]
-        for ah in range(4):
+        for ah in range(0,8,2):
             parts=[]
-            for a in (2*ah,2*ah+1):
-                yp=4*a+b//2; o=384*yp+128*(b%2)
+            for a in range(ah,ah+2):
+                o=384*(4*a+b//2)+128*(b%2)
                 for x in range(4):
                     parts.append(rho[x,:,o:o+256])
             B=jnp.concatenate(parts,axis=0)
-            B=jnp.concatenate([B,B],axis=1)
             res=lax.dot_general(wt,B,(((1,),(1,)),((),())),preferred_element_type=jnp.float32)
-            Z[pl.ds((8*(2*ah)+b)*2*KZ,2*KZ),:]=res[:,:128]
-            Z[pl.ds((8*(2*ah+1)+b)*2*KZ,2*KZ),:]=res[:,128:]
+            res=res[:2*KZ]+res[2*KZ:]
+            for a in range(2):
+                Z[pl.ds((8*(ah+a)+b)*2*KZ,2*KZ),:]=res[:,128*a:128*a+128]
     tw=[[np.exp(-2j*np.pi*b*k/64) for k in range(8)] for b in range(8)]
     def pass1(j,_):
         r0=pl.multiple_of(j*8,8)
@@ -126,7 +126,7 @@
                     re,im=re*c-im*s, re*s+im*c
                 Z[pl.ds((8*k+b)*2*KZ+r0,8),:]=re; Z[pl.ds((8*k+b)*2*KZ+KZ+r0,8),:]=im
         return 0
-    lax.fori_loop(0,KZ//8,pass1,0)
+    lax.fori_loop(0,KZ//8,pass1,0,unroll=True)
     def pass2(j,_):
         r0=pl.multiple_of(j*8,8)
         for k1 in range(8):
@@ -174,7 +174,7 @@
                   pl.BlockSpec(memory_space=pl.ANY),
                   pl.BlockSpec(memory_space=pl.ANY),
                   pl.BlockSpec((32,128),lambda i:(0,0)),
-                  pl.BlockSpec((2,2*KZ,512),lambda i:(0,0,0)),
+                  pl.BlockSpec((2,4*KZ,256),lambda i:(0,0,0)),
                   pl.BlockSpec(memory_space=pl.ANY)],
         out_specs=[pl.BlockSpec((16,16,1024),lambda i:(0,0,0)),pl.BlockSpec((16,128),lambda i:(0,0))],
         scratch_shapes=[pltpu.VMEM((4,32,12288),jnp.bfloat16),

time: 76.7 us -> 75.4 us (0.983)
  Pallas kernels: 14.8 us -> 13.5 us
    pallas_call x1, Pallas kernels: 14.8 us -> 13.5 us  [partial_transform(): pl.pallas_call(transform_kernel, grid=(1,), in_specs=[smem, smem, smem, s...]
where the time goes in v5:
time: 75.4 us; the launch traced here: 75 us
  blocking collectives  45.6 us (60%)
  Pallas kernels  13.5 us (18%)
  waiting for transfers between devices  7.68 us (10%)
  starting transfers between devices  5.86 us (8%)
  other arithmetic  1.02 us (1%)
  local copies, waits for them, and re-layouts  0.91 us (1%)
    all_to_all x1, blocking collectives, body(): lax.all_to_all(payload, ('ph', 'pl'), split_axis=0, concat_axis=0, tiled=...  28.1 us
    pallas_call x1, Pallas kernels, partial_transform(): pl.pallas_call(transform_kernel, grid=(1,), in_specs=[smem, smem, smem, s...  13.5 us
    all_to_all x1, blocking collectives, body(): lax.all_to_all(tiles.reshape(8, 64, 512), ('pl', 'row'), split_axis=0, co...  12.1 us
    all_to_all x1, waiting for transfers between devices, body(): lax.all_to_all(part, ('row', 'col'), split_axis=0, concat_axis=0, tiled=T...  7.68 us
    all_to_all x1, starting transfers between devices, body(): lax.all_to_all(part, ('row', 'col'), split_axis=0, concat_axis=0, tiled=T...  5.86 us
    all_gather x1, blocking collectives, body(): every = lax.all_gather(own, 'col', axis=0)  5.43 us
  transfers between devices with their start and end apart: 1, of which 1 were waited for; matrix products, arithmetic and copies ran while one was open for 1% of the time, Pallas kernels for 0%

profile of v5, /device:TPU:2, one launch (start us, length us, event | category | flops | bytes accessed | tf_op | source)
XLA Modules:
  0.0 75.0 jit_solution(3582390934844489914)
XLA Ops:
  0.0 13.5 %partial_transform.1 = (bf16[16,16,1024]{2,1,0:T(8,128)(2,1)}, f32[16,128]{1,0:T(8,128)}) custom-call(s32[32]{0:T(128)} %val_s.1, s32[32]{0:T(128)} %con_s.1, f32[32]{0:T(128)} %ev_s.1, f32[64]{0:T(128)} %ec_s.1, bf16[32,49152]{1,0:T(8,128)(2,1)} %pv.1, bf16[64,49152]{1,0:T(8,128)(2,1)} %pc.1, s32[32,128]{1,0:T(8,128)} %bitcast.21, ...), custom_call_target="tpu_custom_call" | custom-call | tf_op jit(solution)/shard_map/partial_transform/pallas_call | solution.py:170
  13.5 5.9 %all-to-all-start = ((bf16[16,16,1024]{2,1,0:T(8,128)(2,1)}), bf16[16,16,1024]{2,1,0:T(8,128)(2,1)S(1)}, u32[]{:S(2)}, u32[]{:S(2)}) async-start(bf16[16,16,1024]{2,1,0:T(8,128)(2,1)} %get-tuple-element.7), calls=%async_computation | async-start | bytes 1048576 | tf_op jit(solution)/shard_map/all_to_all | solution.py:202
  19.3 0.8 %slice_reduce_fusion = f32[16]{0:T(128)S(1)} fusion(f32[16,128]{1,0:T(8,128)} %get-tuple-element.8), kind=kLoop, calls=%fused_computation.11 | loop fusion | bytes 128 | tf_op jit(solution)/shard_map/slice | solution.py:205
  20.2 7.7 %all-to-all-done = bf16[16,16,1024]{2,1,0:T(8,128)(2,1)S(1)} async-done(((bf16[16,16,1024]{2,1,0:T(8,128)(2,1)}), bf16[16,16,1024]{2,1,0:T(8,128)(2,1)S(1)}, u32[]{:S(2)}, u32[]{:S(2)}) %all-to-all-start) | async-done | bytes 524320 | tf_op jit(solution)/shard_map/all_to_all | solution.py:202
  27.8 0.1 reduce_sum.21
  27.9 5.4 %all-gather = bf16[64,1024]{1,0:T(8,128)(2,1)S(1)} all-gather(bf16[16,1024]{1,0:T(8,128)(2,1)S(1)} %reduce_sum.21), channel_id=2, replica_groups=mesh['ph'=8,'pl'=2,'row'=4,'col'=4] {'col'}, dimensions={0}, use_global_device_ids=true | all-gather | bytes 163840 | tf_op jit(solution)/shard_map/all_gather | solution.py:204
  33.4 0.1 fusion.2
  33.6 0.1 pad_maximum_fusion
  33.6 28.1 %all_to_all.15 = bf16[16,16,1024]{2,1,0:T(8,128)(2,1)S(1)} all-to-all(bf16[16,16,1024]{2,1,0:T(8,128)(2,1)S(1)} %bitcast.15), channel_id=1, replica_groups=mesh['ph'=8,'pl'=2,'row'=4,'col'=4] {'ph','pl'}, dimensions={0} | all-to-all | bytes 1048576 | tf_op jit(solution)/shard_map/all_to_all | solution.py:209
  61.7 0.3 convolution_convert_fusion
  62.1 12.1 %all_to_all.16 = bf16[8,64,512]{2,1,0:T(8,128)(2,1)S(1)} all-to-all(bf16[8,64,512]{2,1,0:T(8,128)(2,1)S(1)} %bitcast.19), channel_id=1, replica_groups=mesh['ph'=8,'pl'=2,'row'=4,'col'=4] {'pl','row'}, dimensions={0} | all-to-all | bytes 1048576 | tf_op jit(solution)/shard_map/all_to_all | solution.py:211
  74.1 0.1 convert_reduce_fusion
  74.2 0.7 pad_maximum_fusion.1
  (7 shorter events, 0.1 us)
Async XLA Ops:
  13.5 14.4 %all-to-all-start = ((bf16[16,16,1024]{2,1,0:T(8,128)(2,1)}), bf16[16,16,1024]{2,1,0:T(8,128)(2,1)S(1)}, u32[]{:S(2)}, u32[]{:S(2)}) async-start(bf16[16,16,1024]{2,1,0:T(8,128)(2,1)} %get-tuple-element.7), calls=%async_computation | async-start | bytes 1048576 | tf_op jit(solution)/shard_map/all_to_all | solution.py:202

commit v6 on v5

--- a/solution.py
+++ b/solution.py
@@ -42,19 +42,19 @@
 def fft8(v):
     def add(a,b): return (a[0]+b[0],a[1]+b[1])
     def sub(a,b): return (a[0]-b[0],a[1]-b[1])
-    def mi(a): return (a[1],-a[0])
+    def addmi(a,b): return (a[0]+b[1],a[1]-b[0])
+    def submi(a,b): return (a[0]-b[1],a[1]+b[0])
     r=np.float32(math.sqrt(0.5))
     def fft4(x0,x1,x2,x3):
-        a=add(x0,x2); b=sub(x0,x2); c=add(x1,x3); d=mi(sub(x1,x3))
-        return add(a,c),add(b,d),sub(a,c),sub(b,d)
+        a=add(x0,x2); b=sub(x0,x2); c=add(x1,x3); d=sub(x1,x3)
+        return add(a,c),addmi(b,d),sub(a,c),submi(b,d)
     e=fft4(v[0],v[2],v[4],v[6]); o=fft4(v[1],v[3],v[5],v[7])
     o1=((o[1][0]+o[1][1])*r,(o[1][1]-o[1][0])*r)
-    o2=mi(o[2])
-    o3=((o[3][1]-o[3][0])*r,-(o[3][0]+o[3][1])*r)
-    os=(o[0],o1,o2,o3)
-    return [add(e[k],os[k]) for k in range(4)]+[sub(e[k],os[k]) for k in range(4)]
-
-def transform_kernel(val_s, con_s, ev_s, ec_s, pv, pc, gmap, ztab, xtabs, out, wout, va, vb, rho, Z, Z2, GA, GB, xtab, rows_v, kcode, row_s, asem, bsem, xsem, rsem):
+    o3=((o[3][1]-o[3][0])*r,(o[3][0]+o[3][1])*(-r))
+    return [add(e[0],o[0]),add(e[1],o1),addmi(e[2],o[2]),add(e[3],o3),
+            sub(e[0],o[0]),sub(e[1],o1),submi(e[2],o[2]),sub(e[3],o3)]
+
+def transform_kernel(val_s, con_s, ev_s, ec_s, pv, pc, gmap, ztabs, xtabs, out, wout, va, vb, ztab, rho, Z, Z2, GA, GB, xtab, rows_v, kcode, row_s, asem, bsem, zsem, xsem, rsem):
     place=lax.axis_index("row")*4+lax.axis_index("col")
     planes=[(pltpu.make_async_copy(pv.at[:,pl.ds(12288*x,12288)],va.at[x],asem.at[x]),
              pltpu.make_async_copy(pc.at[:,pl.ds(12288*x,12288)],vb.at[x],bsem.at[x])) for x in range(4)]
@@ -63,6 +63,8 @@
         one[1].start()
     fetch=pltpu.make_async_copy(xtabs.at[place],xtab,xsem)
     fetch.start()
+    table=pltpu.make_async_copy(ztabs,ztab,zsem)
+    table.start()
     g=gmap[...]
     q=((g.astype(jnp.float32)+0.5)*np.float32(1.0/GZ)).astype(jnp.int32)
     fz=g-q*GZ; fy=q&63; fx=q>>6
@@ -99,6 +101,7 @@
             res=jnp.dot(sel,src,preferred_element_type=jnp.float32)
             rho[x,:,o:o+CH]=(res[:32]*res[32:]).astype(jnp.bfloat16)
     fetch.wait()
+    table.wait()
     move.wait()
     for b in range(8):
         wt=ztab[b%2]
@@ -174,11 +177,12 @@
                   pl.BlockSpec(memory_space=pl.ANY),
                   pl.BlockSpec(memory_space=pl.ANY),
                   pl.BlockSpec((32,128),lambda i:(0,0)),
-                  pl.BlockSpec((2,4*KZ,256),lambda i:(0,0,0)),
+                  pl.BlockSpec(memory_space=pl.ANY),
                   pl.BlockSpec(memory_space=pl.ANY)],
         out_specs=[pl.BlockSpec((16,16,1024),lambda i:(0,0,0)),pl.BlockSpec((16,128),lambda i:(0,0))],
         scratch_shapes=[pltpu.VMEM((4,32,12288),jnp.bfloat16),
                         pltpu.VMEM((4,64,12288),jnp.bfloat16),
+                        pltpu.VMEM((2,4*KZ,256),jnp.bfloat16),
                         pltpu.VMEM((4,32,12288),jnp.bfloat16),
                         pltpu.VMEM((64*2*KZ,128),jnp.float32),
                         pltpu.VMEM((64*2*KZ,128),jnp.float32),
@@ -190,6 +194,7 @@
                         pltpu.SMEM((32,128),jnp.int32),
                         pltpu.SemaphoreType.DMA((4,)),
                         pltpu.SemaphoreType.DMA((4,)),
+                        pltpu.SemaphoreType.DMA,
                         pltpu.SemaphoreType.DMA,
                         pltpu.SemaphoreType.DMA],
         out_shape=[jax.ShapeDtypeStruct((16,16,1024),jnp.bfloat16),jax.ShapeDtypeStruct((16,128),jnp.float32)],

time: 75.4 us -> 75.2 us (level)
  no operation moved by 1% of the time
where the time goes in v6:
time: 75.2 us; the launch traced here: 74.7 us
  blocking collectives  45.6 us (61%)
  Pallas kernels  13.2 us (18%)
  waiting for transfers between devices  7.68 us (10%)
  starting transfers between devices  5.87 us (8%)
  other arithmetic  1.02 us (1%)
  local copies, waits for them, and re-layouts  0.91 us (1%)
    all_to_all x1, blocking collectives, body(): lax.all_to_all(payload, ('ph', 'pl'), split_axis=0, concat_axis=0, tiled=...  28.1 us
    pallas_call x1, Pallas kernels, partial_transform(): pl.pallas_call(transform_kernel, grid=(1,), in_specs=[smem, smem, smem, s...  13.2 us
    all_to_all x1, blocking collectives, body(): lax.all_to_all(tiles.reshape(8, 64, 512), ('pl', 'row'), split_axis=0, co...  12.1 us
    all_to_all x1, waiting for transfers between devices, body(): lax.all_to_all(part, ('row', 'col'), split_axis=0, concat_axis=0, tiled=T...  7.68 us
    all_to_all x1, starting transfers between devices, body(): lax.all_to_all(part, ('row', 'col'), split_axis=0, concat_axis=0, tiled=T...  5.87 us
    all_gather x1, blocking collectives, body(): every = lax.all_gather(own, 'col', axis=0)  5.43 us
  transfers between devices with their start and end apart: 1, of which 1 were waited for; matrix products, arithmetic and copies ran while one was open for 1% of the time, Pallas kernels for 0%

profile of v6, /device:TPU:2, one launch (start us, length us, event | category | flops | bytes accessed | tf_op | source)
XLA Modules:
  0.0 74.7 jit_solution(14968419012139070682)
XLA Ops:
  0.0 13.2 %partial_transform.1 = (bf16[16,16,1024]{2,1,0:T(8,128)(2,1)}, f32[16,128]{1,0:T(8,128)}) custom-call(s32[32]{0:T(128)} %val_s.1, s32[32]{0:T(128)} %con_s.1, f32[32]{0:T(128)} %ev_s.1, f32[64]{0:T(128)} %ec_s.1, bf16[32,49152]{1,0:T(8,128)(2,1)} %pv.1, bf16[64,49152]{1,0:T(8,128)(2,1)} %pc.1, s32[32,128]{1,0:T(8,128)} %bitcast.21, ...), custom_call_target="tpu_custom_call" | custom-call | tf_op jit(solution)/shard_map/partial_transform/pallas_call | solution.py:173
  13.2 5.9 %all-to-all-start = ((bf16[16,16,1024]{2,1,0:T(8,128)(2,1)}), bf16[16,16,1024]{2,1,0:T(8,128)(2,1)S(1)}, u32[]{:S(2)}, u32[]{:S(2)}) async-start(bf16[16,16,1024]{2,1,0:T(8,128)(2,1)} %get-tuple-element.7), calls=%async_computation | async-start | bytes 1048576 | tf_op jit(solution)/shard_map/all_to_all | solution.py:207
  19.0 0.8 %slice_reduce_fusion = f32[16]{0:T(128)S(1)} fusion(f32[16,128]{1,0:T(8,128)} %get-tuple-element.8), kind=kLoop, calls=%fused_computation.11 | loop fusion | bytes 128 | tf_op jit(solution)/shard_map/slice | solution.py:210
  19.9 7.7 %all-to-all-done = bf16[16,16,1024]{2,1,0:T(8,128)(2,1)S(1)} async-done(((bf16[16,16,1024]{2,1,0:T(8,128)(2,1)}), bf16[16,16,1024]{2,1,0:T(8,128)(2,1)S(1)}, u32[]{:S(2)}, u32[]{:S(2)}) %all-to-all-start) | async-done | bytes 524320 | tf_op jit(solution)/shard_map/all_to_all | solution.py:207
  27.5 0.1 reduce_sum.21
  27.6 5.4 %all-gather = bf16[64,1024]{1,0:T(8,128)(2,1)S(1)} all-gather(bf16[16,1024]{1,0:T(8,128)(2,1)S(1)} %reduce_sum.21), channel_id=2, replica_groups=mesh['ph'=8,'pl'=2,'row'=4,'col'=4] {'col'}, dimensions={0}, use_global_device_ids=true | all-gather | bytes 163840 | tf_op jit(solution)/shard_map/all_gather | solution.py:209
  33.1 0.1 fusion.2
  33.3 0.1 pad_maximum_fusion
  33.3 28.1 %all_to_all.15 = bf16[16,16,1024]{2,1,0:T(8,128)(2,1)S(1)} all-to-all(bf16[16,16,1024]{2,1,0:T(8,128)(2,1)S(1)} %bitcast.15), channel_id=1, replica_groups=mesh['ph'=8,'pl'=2,'row'=4,'col'=4] {'ph','pl'}, dimensions={0} | all-to-all | bytes 1048576 | tf_op jit(solution)/shard_map/all_to_all | solution.py:214
  61.5 0.3 convolution_convert_fusion
  61.8 12.1 %all_to_all.16 = bf16[8,64,512]{2,1,0:T(8,128)(2,1)S(1)} all-to-all(bf16[8,64,512]{2,1,0:T(8,128)(2,1)S(1)} %bitcast.19), channel_id=1, replica_groups=mesh['ph'=8,'pl'=2,'row'=4,'col'=4] {'pl','row'}, dimensions={0} | all-to-all | bytes 1048576 | tf_op jit(solution)/shard_map/all_to_all | solution.py:216
  73.8 0.1 convert_reduce_fusion
  73.9 0.7 pad_maximum_fusion.1
  (7 shorter events, 0.1 us)
Async XLA Ops:
  13.2 14.4 %all-to-all-start = ((bf16[16,16,1024]{2,1,0:T(8,128)(2,1)}), bf16[16,16,1024]{2,1,0:T(8,128)(2,1)S(1)}, u32[]{:S(2)}, u32[]{:S(2)}) async-start(bf16[16,16,1024]{2,1,0:T(8,128)(2,1)} %get-tuple-element.7), calls=%async_computation | async-start | bytes 1048576 | tf_op jit(solution)/shard_map/all_to_all | solution.py:207

commit v7 on v6

--- a/solution.py
+++ b/solution.py
@@ -54,10 +54,12 @@
     return [add(e[0],o[0]),add(e[1],o1),addmi(e[2],o[2]),add(e[3],o3),
             sub(e[0],o[0]),sub(e[1],o1),submi(e[2],o[2]),sub(e[3],o3)]
 
-def transform_kernel(val_s, con_s, ev_s, ec_s, pv, pc, gmap, ztabs, xtabs, out, wout, va, vb, ztab, rho, Z, Z2, GA, GB, xtab, rows_v, kcode, row_s, asem, bsem, zsem, xsem, rsem):
+def transform_kernel(val_s, con_s, ev_s, ec_s, pv, pc, gmaps, ztabs, xtabs, out, wout, va, vb, gmap, ztab, rho, Z, Z2, GA, GB, xtab, rows_v, kcode, row_s, asem, bsem, gsem, zsem, xsem, rsem):
     place=lax.axis_index("row")*4+lax.axis_index("col")
     planes=[(pltpu.make_async_copy(pv.at[:,pl.ds(12288*x,12288)],va.at[x],asem.at[x]),
              pltpu.make_async_copy(pc.at[:,pl.ds(12288*x,12288)],vb.at[x],bsem.at[x])) for x in range(4)]
+    small=pltpu.make_async_copy(gmaps,gmap,gsem)
+    small.start()
     for one in planes:
         one[0].start()
         one[1].start()
@@ -65,6 +67,7 @@
     fetch.start()
     table=pltpu.make_async_copy(ztabs,ztab,zsem)
     table.start()
+    small.wait()
     g=gmap[...]
     q=((g.astype(jnp.float32)+0.5)*np.float32(1.0/GZ)).astype(jnp.int32)
     fz=g-q*GZ; fy=q&63; fx=q>>6
@@ -176,12 +179,13 @@
         in_specs=[smem,smem,smem,smem,
                   pl.BlockSpec(memory_space=pl.ANY),
                   pl.BlockSpec(memory_space=pl.ANY),
-                  pl.BlockSpec((32,128),lambda i:(0,0)),
+                  pl.BlockSpec(memory_space=pl.ANY),
                   pl.BlockSpec(memory_space=pl.ANY),
                   pl.BlockSpec(memory_space=pl.ANY)],
         out_specs=[pl.BlockSpec((16,16,1024),lambda i:(0,0,0)),pl.BlockSpec((16,128),lambda i:(0,0))],
         scratch_shapes=[pltpu.VMEM((4,32,12288),jnp.bfloat16),
                         pltpu.VMEM((4,64,12288),jnp.bfloat16),
+                        pltpu.VMEM((32,128),jnp.int32),
                         pltpu.VMEM((2,4*KZ,256),jnp.bfloat16),
                         pltpu.VMEM((4,32,12288),jnp.bfloat16),
                         pltpu.VMEM((64*2*KZ,128),jnp.float32),
@@ -194,6 +198,7 @@
                         pltpu.SMEM((32,128),jnp.int32),
                         pltpu.SemaphoreType.DMA((4,)),
                         pltpu.SemaphoreType.DMA((4,)),
+                        pltpu.SemaphoreType.DMA,
                         pltpu.SemaphoreType.DMA,
                         pltpu.SemaphoreType.DMA,
                         pltpu.SemaphoreType.DMA],

time: 75.2 us -> 75.9 us (level)
  Pallas kernels: 13.2 us -> 14 us
    pallas_call x1, Pallas kernels: 13.2 us -> 14 us  [partial_transform(): pl.pallas_call(transform_kernel, grid=(1,), in_specs=[smem, smem, smem, s...]
where the time goes in v7:
time: 75.9 us; the launch traced here: 75.5 us
  blocking collectives  45.6 us (60%)
  Pallas kernels  14 us (18%)
  waiting for transfers between devices  7.68 us (10%)
  starting transfers between devices  5.85 us (8%)
  other arithmetic  1.02 us (1%)
  local copies, waits for them, and re-layouts  0.91 us (1%)
    all_to_all x1, blocking collectives, body(): lax.all_to_all(payload, ('ph', 'pl'), split_axis=0, concat_axis=0, tiled=...  28.1 us
    pallas_call x1, Pallas kernels, partial_transform(): pl.pallas_call(transform_kernel, grid=(1,), in_specs=[smem, smem, smem, s...  14 us
    all_to_all x1, blocking collectives, body(): lax.all_to_all(tiles.reshape(8, 64, 512), ('pl', 'row'), split_axis=0, co...  12.1 us
    all_to_all x1, waiting for transfers between devices, body(): lax.all_to_all(part, ('row', 'col'), split_axis=0, concat_axis=0, tiled=T...  7.68 us
    all_to_all x1, starting transfers between devices, body(): lax.all_to_all(part, ('row', 'col'), split_axis=0, concat_axis=0, tiled=T...  5.85 us
    all_gather x1, blocking collectives, body(): every = lax.all_gather(own, 'col', axis=0)  5.43 us
  transfers between devices with their start and end apart: 1, of which 1 were waited for; matrix products, arithmetic and copies ran while one was open for 1% of the time, Pallas kernels for 0%

profile of v7, /device:TPU:2, one launch (start us, length us, event | category | flops | bytes accessed | tf_op | source)
XLA Modules:
  0.0 75.5 jit_solution(11183511914747099095)
XLA Ops:
  0.0 14.0 %partial_transform.1 = (bf16[16,16,1024]{2,1,0:T(8,128)(2,1)}, f32[16,128]{1,0:T(8,128)}) custom-call(s32[32]{0:T(128)} %val_s.1, s32[32]{0:T(128)} %con_s.1, f32[32]{0:T(128)} %ev_s.1, f32[64]{0:T(128)} %ec_s.1, bf16[32,49152]{1,0:T(8,128)(2,1)} %pv.1, bf16[64,49152]{1,0:T(8,128)(2,1)} %pc.1, s32[32,128]{1,0:T(8,128)} %bitcast.21, ...), custom_call_target="tpu_custom_call" | custom-call | tf_op jit(solution)/shard_map/partial_transform/pallas_call | solution.py:176
  14.0 5.9 %all-to-all-start = ((bf16[16,16,1024]{2,1,0:T(8,128)(2,1)}), bf16[16,16,1024]{2,1,0:T(8,128)(2,1)S(1)}, u32[]{:S(2)}, u32[]{:S(2)}) async-start(bf16[16,16,1024]{2,1,0:T(8,128)(2,1)} %get-tuple-element.7), calls=%async_computation | async-start | bytes 1048576 | tf_op jit(solution)/shard_map/all_to_all | solution.py:212
  19.8 0.8 %slice_reduce_fusion = f32[16]{0:T(128)S(1)} fusion(f32[16,128]{1,0:T(8,128)} %get-tuple-element.8), kind=kLoop, calls=%fused_computation.11 | loop fusion | bytes 128 | tf_op jit(solution)/shard_map/slice | solution.py:215
  20.7 7.7 %all-to-all-done = bf16[16,16,1024]{2,1,0:T(8,128)(2,1)S(1)} async-done(((bf16[16,16,1024]{2,1,0:T(8,128)(2,1)}), bf16[16,16,1024]{2,1,0:T(8,128)(2,1)S(1)}, u32[]{:S(2)}, u32[]{:S(2)}) %all-to-all-start) | async-done | bytes 524320 | tf_op jit(solution)/shard_map/all_to_all | solution.py:212
  28.3 0.1 reduce_sum.21
  28.4 5.4 %all-gather = bf16[64,1024]{1,0:T(8,128)(2,1)S(1)} all-gather(bf16[16,1024]{1,0:T(8,128)(2,1)S(1)} %reduce_sum.21), channel_id=2, replica_groups=mesh['ph'=8,'pl'=2,'row'=4,'col'=4] {'col'}, dimensions={0}, use_global_device_ids=true | all-gather | bytes 163840 | tf_op jit(solution)/shard_map/all_gather | solution.py:214
  33.9 0.1 fusion.2
  34.1 0.1 pad_maximum_fusion
  34.1 28.1 %all_to_all.15 = bf16[16,16,1024]{2,1,0:T(8,128)(2,1)S(1)} all-to-all(bf16[16,16,1024]{2,1,0:T(8,128)(2,1)S(1)} %bitcast.15), channel_id=1, replica_groups=mesh['ph'=8,'pl'=2,'row'=4,'col'=4] {'ph','pl'}, dimensions={0} | all-to-all | bytes 1048576 | tf_op jit(solution)/shard_map/all_to_all | solution.py:219
  62.3 0.3 convolution_convert_fusion
  62.6 12.1 %all_to_all.16 = bf16[8,64,512]{2,1,0:T(8,128)(2,1)S(1)} all-to-all(bf16[8,64,512]{2,1,0:T(8,128)(2,1)S(1)} %bitcast.19), channel_id=1, replica_groups=mesh['ph'=8,'pl'=2,'row'=4,'col'=4] {'pl','row'}, dimensions={0} | all-to-all | bytes 1048576 | tf_op jit(solution)/shard_map/all_to_all | solution.py:221
  74.6 0.1 convert_reduce_fusion
  74.7 0.7 pad_maximum_fusion.1
  (7 shorter events, 0.1 us)
Async XLA Ops:
  14.0 14.3 %all-to-all-start = ((bf16[16,16,1024]{2,1,0:T(8,128)(2,1)}), bf16[16,16,1024]{2,1,0:T(8,128)(2,1)S(1)}, u32[]{:S(2)}, u32[]{:S(2)}) async-start(bf16[16,16,1024]{2,1,0:T(8,128)(2,1)} %get-tuple-element.7), calls=%async_computation | async-start | bytes 1048576 | tf_op jit(solution)/shard_map/all_to_all | solution.py:212
